TPU v7x, 32 devices: a whole 2x2x4 slice. The times are simulated.
32 devices in a mesh: win: 4 (over y, x), head: 8 (over z, core).
Axes of the slice: x: 2, y: 2, z: 4, core: 2. Of those that a mesh axis runs over, the one named last changes fastest.
Arguments:
- section_rows: bfloat16 [384, 100, 4, 256], P('win', None, None, 'head'), may hold values from -6 to 6
- reduce_weight: bfloat16 [4, 256, 512], replicated, may hold values from -0.1875 to 0.1875
- norm0_gain: float32 [4, 256], replicated, may hold values from 0.5 to 1.5
- norm0_bias: float32 [4, 256], replicated, may hold values from -1.75 to 1.75
- norm1_gain: float32 [512], replicated, may hold values from 0.5 to 1.5
- norm1_bias: float32 [512], replicated, may hold values from -1.75 to 1.75
- qkv_weight: bfloat16 [512, 1536], replicated, may hold values from -0.25 to 0.25
- q_bias: float32 [512], replicated, may hold values from -3 to 3
- v_bias: float32 [512], replicated, may hold values from -3 to 3
- rel_table: float32 [16, 361], replicated, may hold values from -6 to 6
- proj_weight: bfloat16 [512, 512], replicated, may hold values from -0.75 to 0.75
- proj_bias: float32 [512], replicated, may hold values from -1.75 to 1.75
- norm2_gain: float32 [512], replicated, may hold values from 0.5 to 1.5
- norm2_bias: float32 [512], replicated, may hold values from -1.75 to 1.75
- fc1_weight: bfloat16 [512, 2048], replicated, may hold values from -0.25 to 0.25
- fc1_bias: float32 [2048], replicated, may hold values from -3 to 3
- fc2_weight: bfloat16 [2048, 512], replicated, may hold values from -0.25 to 0.25
- fc2_bias: float32 [512], replicated, may hold values from -1.75 to 1.75
- window_valid: int32 [384], P(('win', 'head')), may hold values 0 or 1
- cotangent: bfloat16 [384, 100, 512], P(('win', 'head')), may hold values from -6 to 6
Outputs:
- block_out: bfloat16 [384, 100, 512], P(('win', 'head'))
- section_grad: bfloat16 [384, 100, 4, 256], P('win', None, None, 'head')
- reduce_grad: float32 [4, 256, 512], P(None, 'head')
- norm0_gain_grad: float32 [4, 256], P(None, 'head')
- norm0_bias_grad: float32 [4, 256], P(None, 'head')
- norm1_gain_grad: float32 [512], P(('win', 'head'))
- norm1_bias_grad: float32 [512], P(('win', 'head'))
- qkv_grad: float32 [512, 1536], P(('win', 'head'))
- q_bias_grad: float32 [512], P(('win', 'head'))
- v_bias_grad: float32 [512], P(('win', 'head'))
- table_grad: float32 [16, 361], replicated
- proj_grad: float32 [512, 512], P(('win', 'head'))
- proj_bias_grad: float32 [512], P(('win', 'head'))
- norm2_gain_grad: float32 [512], P(('win', 'head'))
- norm2_bias_grad: float32 [512], P(('win', 'head'))
- fc1_grad: float32 [512, 2048], P(('win', 'head'))
- fc1_bias_grad: float32 [2048], P(('win', 'head'))
- fc2_grad: float32 [2048, 512], P(('win', 'head'))
- fc2_bias_grad: float32 [512], P(('win', 'head'))
All inputs are finite; a program needn't handle non-finite values. No bound on the sum of `window_valid` on one device may be relied on, other than what follows from the above.
Results may differ from a plain program's by a relative error of at most 0.02.
Values may be sent and summed in bfloat16 or wider, within the bound.
A program may use at most 192 MiB of HBM per device.

v0:
```python
import jax
import jax.numpy as jnp
from jax import lax
from jax.sharding import PartitionSpec as P

C2 = 256
DM = 512
HEADS = 16
HD = 32
WIN = 10
WT = 100
RELS = 361


epsilon = 1e-05


def layer_norm(values, gain, shift):
    average = jnp.mean(values, axis=-1, keepdims=True)
    centred = values - average
    variance = jnp.mean(centred * centred, axis=-1, keepdims=True)
    return centred * lax.rsqrt(variance + epsilon) * gain + shift


def norm_back(values, gain, shift, upstream):
    unused, pullback = jax.vjp(layer_norm, values, gain, shift)
    return pullback(upstream)


def exact_gelu(values):
    return jax.nn.gelu(values, approximate=False)


def relative_onehot():
    positions = jnp.arange(WT, dtype=jnp.int32)
    pos_row = positions // WIN
    pos_col = positions % WIN
    rel_index = (pos_row[:, None] - pos_row[None, :] + WIN - 1) * (2 * WIN - 1) + (
        pos_col[:, None] - pos_col[None, :] + WIN - 1
    )
    offsets = jnp.arange(RELS, dtype=jnp.int32)
    return (rel_index[:, :, None] == offsets[None, None, :]).astype(jnp.float32)


def local(
    section_rows,
    reduce_weight,
    norm0_gain,
    norm0_bias,
    norm1_gain,
    norm1_bias,
    qkv_weight,
    q_bias,
    v_bias,
    rel_table,
    proj_weight,
    proj_bias,
    norm2_gain,
    norm2_bias,
    fc1_weight,
    fc1_bias,
    fc2_weight,
    fc2_bias,
    window_valid,
    cotangent,
):
    group_windows, tokens, quads, share = section_rows.shape
    windows = cotangent.shape[0]
    rows = windows * tokens
    width = quads * C2
    full_weight = reduce_weight.reshape(width, DM)
    gathered = lax.all_to_all(section_rows, "head", split_axis=0, concat_axis=3, tiled=True)
    merged = gathered.astype(jnp.float32).reshape(rows, width)
    normed_low = layer_norm(merged, norm0_gain.reshape(width), norm0_bias.reshape(width)).astype(
        jnp.bfloat16
    )
    resid = jnp.dot(normed_low, full_weight, preferred_element_type=jnp.float32)
    first_low = layer_norm(resid, norm1_gain, norm1_bias).astype(jnp.bfloat16)
    packed = jnp.dot(first_low, qkv_weight, preferred_element_type=jnp.float32)
    query = (packed[:, :DM] + q_bias).astype(jnp.bfloat16).reshape(windows, tokens, HEADS, HD)
    key_heads = packed[:, DM : 2 * DM].astype(jnp.bfloat16).reshape(windows, tokens, HEADS, HD)
    value_heads = (
        (packed[:, 2 * DM :] + v_bias).astype(jnp.bfloat16).reshape(windows, tokens, HEADS, HD)
    )
    onehot = relative_onehot()
    pos_bias = jnp.einsum("ijr,hr->hij", onehot, rel_table, precision=lax.Precision.HIGHEST)
    scale = HD ** (-0.5)
    scores = (
        jnp.einsum("wihd,wjhd->whij", query, key_heads, preferred_element_type=jnp.float32) * scale
        + pos_bias[None]
    )
    peak = jnp.max(scores, axis=-1, keepdims=True)
    expo = jnp.exp(scores - peak)
    expo_sum = jnp.sum(expo, axis=-1, keepdims=True)
    log_total = peak + jnp.log(expo_sum)
    probs_low = (expo / expo_sum).astype(jnp.bfloat16)
    attended = jnp.einsum(
        "whij,wjhd->wihd", probs_low, value_heads, preferred_element_type=jnp.float32
    )
    attended_low = attended.astype(jnp.bfloat16).reshape(rows, DM)
    second = (
        resid + jnp.dot(attended_low, proj_weight, preferred_element_type=jnp.float32) + proj_bias
    )
    second_low = layer_norm(second, norm2_gain, norm2_bias).astype(jnp.bfloat16)
    hidden = jnp.dot(second_low, fc1_weight, preferred_element_type=jnp.float32) + fc1_bias
    activated_low = exact_gelu(hidden).astype(jnp.bfloat16)
    result = (
        second + jnp.dot(activated_low, fc2_weight, preferred_element_type=jnp.float32) + fc2_bias
    )
    mask_rows = jnp.repeat(window_valid, tokens)[:, None] > 0
    block_out = jnp.where(mask_rows, result, 0.0).astype(jnp.bfloat16).reshape(windows, tokens, DM)
    upstream = jnp.where(mask_rows, cotangent.reshape(rows, DM), jnp.zeros((), jnp.bfloat16))
    grad_fc2 = jnp.dot(activated_low.T, upstream, preferred_element_type=jnp.float32)
    grad_fc2_bias = jnp.sum(upstream.astype(jnp.float32), axis=0)
    grad_act = jnp.dot(upstream, fc2_weight.T, preferred_element_type=jnp.float32)
    unused, gelu_pull = jax.vjp(exact_gelu, hidden)
    grad_hidden = gelu_pull(grad_act)[0].astype(jnp.bfloat16)
    grad_fc1 = jnp.dot(second_low.T, grad_hidden, preferred_element_type=jnp.float32)
    grad_fc1_bias = jnp.sum(grad_hidden.astype(jnp.float32), axis=0)
    grad_second_norm = jnp.dot(grad_hidden, fc1_weight.T, preferred_element_type=jnp.float32)
    grad_second, grad_norm2_gain, grad_norm2_bias = norm_back(
        second, norm2_gain, norm2_bias, grad_second_norm
    )
    grad_second = grad_second + upstream.astype(jnp.float32)
    branch_low = grad_second.astype(jnp.bfloat16)
    grad_proj = jnp.dot(attended_low.T, branch_low, preferred_element_type=jnp.float32)
    grad_proj_bias = jnp.sum(branch_low.astype(jnp.float32), axis=0)
    grad_attended = jnp.dot(branch_low, proj_weight.T, preferred_element_type=jnp.float32)
    grad_attended = grad_attended.astype(jnp.bfloat16).reshape(windows, tokens, HEADS, HD)
    again = (
        jnp.einsum("wihd,wjhd->whij", query, key_heads, preferred_element_type=jnp.float32) * scale
        + pos_bias[None]
    )
    probs = jnp.exp(again - log_total)
    probs_again = probs.astype(jnp.bfloat16)
    grad_probs = jnp.einsum(
        "wihd,wjhd->whij", grad_attended, value_heads, preferred_element_type=jnp.float32
    )
    grad_values = jnp.einsum(
        "whij,wihd->wjhd", probs_again, grad_attended, preferred_element_type=jnp.float32
    )
    grad_scores = probs * (grad_probs - jnp.sum(probs * grad_probs, axis=-1, keepdims=True))
    grad_table = jnp.einsum(
        "hij,ijr->hr", jnp.sum(grad_scores, axis=0), onehot, precision=lax.Precision.HIGHEST
    )
    grad_raw = (grad_scores * scale).astype(jnp.bfloat16)
    grad_query = jnp.einsum(
        "whij,wjhd->wihd", grad_raw, key_heads, preferred_element_type=jnp.float32
    )
    grad_key = jnp.einsum("whij,wihd->wjhd", grad_raw, query, preferred_element_type=jnp.float32)
    grad_query = grad_query.astype(jnp.bfloat16).reshape(rows, DM)
    grad_key = grad_key.astype(jnp.bfloat16).reshape(rows, DM)
    grad_value_low = grad_values.astype(jnp.bfloat16).reshape(rows, DM)
    grad_packed = jnp.concatenate([grad_query, grad_key, grad_value_low], axis=1)
    grad_qkv = jnp.dot(first_low.T, grad_packed, preferred_element_type=jnp.float32)
    grad_q_bias = jnp.sum(grad_query.astype(jnp.float32), axis=0)
    grad_v_bias = jnp.sum(grad_value_low.astype(jnp.float32), axis=0)
    grad_first = jnp.dot(grad_packed, qkv_weight.T, preferred_element_type=jnp.float32)
    grad_resid, grad_norm1_gain, grad_norm1_bias = norm_back(
        resid, norm1_gain, norm1_bias, grad_first
    )
    resid_low = (grad_resid + grad_second).astype(jnp.bfloat16)
    grad_weight = jnp.dot(normed_low.T, resid_low, preferred_element_type=jnp.float32).reshape(
        quads, C2, DM
    )
    grad_normed = jnp.dot(resid_low, full_weight.T, preferred_element_type=jnp.float32)
    grad_merged, grad_gain_zero, grad_shift_zero = norm_back(
        merged, norm0_gain.reshape(width), norm0_bias.reshape(width), grad_normed
    )
    grad_rows = grad_merged.astype(jnp.bfloat16).reshape(windows, tokens, quads, C2)
    section_grad = lax.all_to_all(grad_rows, "head", split_axis=3, concat_axis=0, tiled=True)
    head_sums = (
        lax.psum_scatter(
            grad_weight.astype(jnp.bfloat16), "head", scatter_dimension=1, tiled=True
        ).astype(jnp.float32),
        lax.psum_scatter(
            grad_gain_zero.reshape(quads, C2).astype(jnp.bfloat16),
            "head",
            scatter_dimension=1,
            tiled=True,
        ).astype(jnp.float32),
        lax.psum_scatter(
            grad_shift_zero.reshape(quads, C2).astype(jnp.bfloat16),
            "head",
            scatter_dimension=1,
            tiled=True,
        ).astype(jnp.float32),
    )
    reduce_grad, norm0_gain_grad, norm0_bias_grad = (
        lax.psum(head_sums[0].astype(jnp.bfloat16), "win").astype(jnp.float32),
        lax.psum(head_sums[1].astype(jnp.bfloat16), "win").astype(jnp.float32),
        lax.psum(head_sums[2].astype(jnp.bfloat16), "win").astype(jnp.float32),
    )
    block_sums = (
        lax.psum_scatter(grad_qkv, ("win", "head"), scatter_dimension=0, tiled=True),
        lax.psum_scatter(grad_proj, ("win", "head"), scatter_dimension=0, tiled=True),
        lax.psum_scatter(grad_fc1, ("win", "head"), scatter_dimension=0, tiled=True),
        lax.psum_scatter(grad_fc2, ("win", "head"), scatter_dimension=0, tiled=True),
        lax.psum_scatter(grad_q_bias, ("win", "head"), scatter_dimension=0, tiled=True),
        lax.psum_scatter(grad_v_bias, ("win", "head"), scatter_dimension=0, tiled=True),
        lax.psum_scatter(grad_proj_bias, ("win", "head"), scatter_dimension=0, tiled=True),
        lax.psum_scatter(grad_fc1_bias, ("win", "head"), scatter_dimension=0, tiled=True),
        lax.psum_scatter(grad_fc2_bias, ("win", "head"), scatter_dimension=0, tiled=True),
        lax.psum_scatter(grad_norm1_gain, ("win", "head"), scatter_dimension=0, tiled=True),
        lax.psum_scatter(grad_norm1_bias, ("win", "head"), scatter_dimension=0, tiled=True),
        lax.psum_scatter(grad_norm2_gain, ("win", "head"), scatter_dimension=0, tiled=True),
        lax.psum_scatter(grad_norm2_bias, ("win", "head"), scatter_dimension=0, tiled=True),
    )
    table_grad = lax.psum(grad_table, ("win", "head"))
    (
        qkv_grad,
        proj_grad,
        fc1_grad,
        fc2_grad,
        q_bias_grad,
        v_bias_grad,
        proj_bias_grad,
        fc1_bias_grad,
        fc2_bias_grad,
        norm1_gain_grad,
        norm1_bias_grad,
        norm2_gain_grad,
        norm2_bias_grad,
    ) = block_sums
    return (
        block_out,
        section_grad,
        reduce_grad,
        norm0_gain_grad,
        norm0_bias_grad,
        norm1_gain_grad,
        norm1_bias_grad,
        qkv_grad,
        q_bias_grad,
        v_bias_grad,
        table_grad,
        proj_grad,
        proj_bias_grad,
        norm2_gain_grad,
        norm2_bias_grad,
        fc1_grad,
        fc1_bias_grad,
        fc2_grad,
        fc2_bias_grad,
    )


def solution(mesh):
    in_specs = (
        P("win", None, None, "head"),
        P(),
        P(),
        P(),
        P(),
        P(),
        P(),
        P(),
        P(),
        P(),
        P(),
        P(),
        P(),
        P(),
        P(),
        P(),
        P(),
        P(),
        P(("win", "head")),
        P(("win", "head"), None, None),
    )
    out_specs = (
        P(("win", "head"), None, None),
        P("win", None, None, "head"),
        P(None, "head", None),
        P(None, "head"),
        P(None, "head"),
        P(("win", "head")),
        P(("win", "head")),
        P(("win", "head"), None),
        P(("win", "head")),
        P(("win", "head")),
        P(),
        P(("win", "head"), None),
        P(("win", "head")),
        P(("win", "head")),
        P(("win", "head")),
        P(("win", "head"), None),
        P(("win", "head")),
        P(("win", "head"), None),
        P(("win", "head")),
    )
    return jax.shard_map(local, mesh=mesh, in_specs=in_specs, out_specs=out_specs, check_vma=False)
```

profile of v0, /device:TPU:0, one launch (start us, length us, event | category | flops | bytes accessed | tf_op | source)
XLA Modules:
  0.0 1005.6 jit_solution(2066542064076320186)
XLA Ops:
  14.6 12.1 %fusion.54 = f32[16,100,100]{2,0,1:T(8,128)} fusion(s32[100,100]{1,0:T(8,128)S(1)} %add_add_fusion.3, f32[16,361]{1,0:T(8,128)S(1)} %copy-done.51), kind=kOutput, calls=%fused_computation.96 | convolution fusion | flops 696729984 | bytes 703104 | tf_op jit(solution)/shard_map/ijr,hr->hij/dot_general | solution.py:86
  32.5 52.9 %all-to-all-done = bf16[96,100,4,32]{1,3,2,0:T(8,128)(2,1)} async-done(((bf16[96,100,4,32]{1,3,2,0:T(8,128)(2,1)}), bf16[96,100,4,32]{1,3,2,0:T(8,128)(2,1)}, u32[]{:S(2)}, u32[]{:S(2)}) %all-to-all-start) | async-done | bytes 2457632 | tf_op jit(solution)/shard_map/all_to_all | solution.py:72
  97.8 9.2 add_convert_fusion.1
  107.0 7.4 convert_element_type.151
  172.0 26.3 %multiply_convert_fusion.1 = (bf16[1200,2048]{1,0:T(8,128)(2,1)}, f32[1200,2048]{1,0:T(8,128)}, f32[1200,2048]{1,0:T(8,128)}) fusion(f32[2048]{0:T(1024)S(1)} %copy-done.52, bf16[512,2048]{1,0:T(8,128)(2,1)S(1)} %copy-done, f32[1200,512]{1,0:T(8,128)S(1)} %get-tuple-element.60, f32[512]{0:T(512)S(1)} %copy-done.38, f32[512]{0:T(512)S(1)} %copy-done.34, ...), kind=kOutput, calls=%fused_computation.16 | convolution fusion | flops 2681856000 | bytes 29152640 | tf_op jit(solution)/shard_map/dot_general | solution.py:105
  198.3 9.9 convert_reduce_fusion
  224.3 8.3 fusion.57
  232.5 7.9 convert_reduce_fusion.1
  240.4 20.7 %fusion.87 = (f32[16,100,100]{1,2,0:T(8,128)}, f32[12,16,100,100]{2,3,1,0:T(8,128)}) fusion(f32[12,16,100,100]{2,3,1,0:T(8,128)} %fusion.57, f32[12,16,100,100]{2,3,1,0:T(8,128)} %copy-done.2, f32[12,16,100]{2,1,0:T(8,128)S(1)} %log_add_fusion, f32[16,100,100]{1,2,0:T(8,128)S(1)} %copy.112), kind=kOutput, calls=%fused_computation.151 | output fusion | flops 19059300 | bytes 24396800 | tf_op jit(solution)/shard_map/sub | solution.py:142
  261.2 7.9 fusion.52
  272.9 8.3 copy.182
  305.1 8.9 reshape.367
  332.8 29.8 %reduce-scatter.12.cloned.1.call-done = bf16[4,32,512]{2,1,0:T(8,128)(2,1)} async-done(((bf16[4,256,512]{2,1,0:T(8,128)(2,1)}), bf16[4,32,512]{2,1,0:T(8,128)(2,1)}) %reduce-scatter.12.cloned.1.call-update) | async-done | bytes 131088 | tf_op jit(solution)/shard_map/reduce_scatter | solution.py:173
  365.9 7.1 fusion.77
  373.3 8.4 fusion.79
  381.7 7.4 fusion.76
  401.7 6.6 copy.129
  414.1 7.6 fusion.66
  421.7 84.3 %all-reduce.9 = (f32[512]{0:T(512)S(1)}, f32[512]{0:T(512)S(1)}, f32[512]{0:T(512)S(1)}, f32[512]{0:T(512)S(1)}, f32[16,361]{1,0:T(8,128)}, /*index=5*/f32[512]{...) all-reduce(f32[512]{0:T(512)S(1)} %get-tuple-element.23, ...), channel_id=5, replica_groups=mesh['win'=4,'head'=8] {'win','head'}, use_global_device_ids=true, to_apply=%region_24.25.clone | all-reduce | flops 11920 | bytes 95360
  520.5 10.0 all-reduce.10
  538.7 68.9 %reduce-scatter.16.cloned.1.call-done = f32[16,512]{1,0:T(8,128)} async-done(((f32[512,512]{1,0:T(8,128)}), f32[16,512]{1,0:T(8,128)}) %reduce-scatter.16.cloned.1.call-update) | async-done | bytes 32784 | tf_op jit(solution)/shard_map/reduce_scatter | solution.py:196
  607.5 103.9 %reduce-scatter.14.cloned.1.call-done = f32[16,1536]{1,0:T(8,128)} async-done(((f32[512,1536]{1,0:T(8,128)}), f32[16,1536]{1,0:T(8,128)}) %reduce-scatter.14.cloned.1.call-update) | async-done | bytes 98320 | tf_op jit(solution)/shard_map/reduce_scatter | solution.py:195
  711.4 143.8 %reduce-scatter.18.cloned.1.call-done = f32[16,2048]{1,0:T(8,128)} async-done(((f32[512,2048]{1,0:T(8,128)}), f32[16,2048]{1,0:T(8,128)}) %reduce-scatter.18.cloned.1.call-update) | async-done | bytes 131088 | tf_op jit(solution)/shard_map/reduce_scatter | solution.py:197
  855.2 143.1 %reduce-scatter.20.cloned.1.call-done = f32[64,512]{1,0:T(8,128)} async-done(((f32[2048,512]{1,0:T(8,128)}), f32[64,512]{1,0:T(8,128)}) %reduce-scatter.20.cloned.1.call-update) | async-done | bytes 131088 | tf_op jit(solution)/shard_map/reduce_scatter | solution.py:198
  (236 shorter events, 189.7 us)
Async XLA Ops:
  7.2 164.8 %copy-start = (bf16[512,2048]{1,0:T(8,128)(2,1)S(1)}, bf16[512,2048]{1,0:T(8,128)(2,1)}, u32[]{:S(2)}) copy-start(bf16[512,2048]{1,0:T(8,128)(2,1)} %param.34) | copy-start | bytes 6291460
  7.2 7.4 copy-start.51
  7.2 78.1 %all-to-all-start = ((bf16[96,100,4,32]{1,3,2,0:T(8,128)(2,1)}), bf16[96,100,4,32]{1,3,2,0:T(8,128)(2,1)}, u32[]{:S(2)}, u32[]{:S(2)}) async-start(bf16[96,100,4,32]{1,3,2,0:T(8,128)(2,1)} %param.20), calls=%async_computation | async-start | bytes 6291456 | tf_op jit(solution)/shard_map/all_to_all | solution.py:72
  13.7 348.9 %reduce-scatter.12.cloned.1.call-start = ((), (), s32[]{:S(2)}) async-start(), calls=%async_computation.9 | async-start | bytes 1179648 | tf_op jit(solution)/shard_map/reduce_scatter | solution.py:173
  14.6 13.6 %copy-start.56 = (s32[12]{0:T(128)S(1)}, s32[12]{0:T(128)}, u32[]{:S(2)}) copy-start(s32[12]{0:T(128)} %param.38) | copy-start | bytes 148
  161.5 6.7 copy-start.42
  171.4 40.3 %copy-start.4 = (f32[1200,512]{1,0:T(8,128)}, f32[1200,512]{1,0:T(8,128)S(1)}, u32[]{:S(2)}) copy-start(f32[1200,512]{1,0:T(8,128)S(1)} %get-tuple-element.60) | copy-start | bytes 7372804
  172.0 26.3 %copy-start.12 = (bf16[1200,512]{1,0:T(8,128)(2,1)S(1)}, bf16[1200,512]{1,0:T(8,128)(2,1)}, u32[]{:S(2)}) copy-start(bf16[1200,512]{1,0:T(8,128)(2,1)} %reshape.361) | copy-start | bytes 3686404
  172.0 26.3 %copy-start.47 = (bf16[2048,512]{1,0:T(8,128)(2,1)S(1)}, bf16[2048,512]{1,0:T(8,128)(2,1)}, u32[]{:S(2)}) copy-start(bf16[2048,512]{1,0:T(8,128)(2,1)} %param.36) | copy-start | bytes 6291460
  240.4 20.7 %copy-start.10 = (bf16[12,100,16,32]{1,0,3,2:T(8,128)(2,1)S(1)}, bf16[12,100,16,32]{1,0,3,2:T(8,128)(2,1)}, u32[]{:S(2)}) copy-start(bf16[12,100,16,32]{1,0,3,2:T(8,128)(2,1)} %reshape.357) | copy-start | bytes 3686404
  261.2 8.0 copy-start.3
  261.2 8.0 copy-start.11
  272.9 8.3 copy-start.15
  328.6 34.1 %copy-start.17 = (bf16[1200,512]{0,1:T(8,128)(2,1)S(1)}, bf16[1200,512]{0,1:T(8,128)(2,1)}, u32[]{:S(2)}) copy-start(bf16[1200,512]{0,1:T(8,128)(2,1)} %reshape.359) | copy-start | bytes 3686404
  331.1 187.8 %reduce-scatter.22.cloned.1.call-start = ((), (), s32[]{:S(2)}) async-start(), calls=%async_computation.15 | async-start | bytes 73728
  332.0 187.8 %reduce-scatter.24.cloned.1.call-start = ((), (), s32[]{:S(2)}) async-start(), calls=%async_computation.16 | async-start | bytes 73728
  332.8 198.9 %all-reduce.13.cloned.1.call-start = ((), (), s32[]{:S(2)}) async-start(), calls=%async_computation.10 | async-start | bytes 262144 | tf_op jit(solution)/shard_map/psum | solution.py:190
  362.6 244.9 %reduce-scatter.16.cloned.1.call-start = ((), (), s32[]{:S(2)}) async-start(), calls=%async_computation.12 | async-start | bytes 1081344 | tf_op jit(solution)/shard_map/reduce_scatter | solution.py:196
  365.8 345.6 %reduce-scatter.14.cloned.1.call-start = ((), (), s32[]{:S(2)}) async-start(), calls=%async_computation.11 | async-start | bytes 3244032 | tf_op jit(solution)/shard_map/reduce_scatter | solution.py:195
  373.0 482.2 %reduce-scatter.18.cloned.1.call-start = ((), (), s32[]{:S(2)}) async-start(), calls=%async_computation.13 | async-start | bytes 4325376 | tf_op jit(solution)/shard_map/reduce_scatter | solution.py:197
  381.7 616.7 %reduce-scatter.20.cloned.1.call-start = ((), (), s32[]{:S(2)}) async-start(), calls=%async_computation.14 | async-start | bytes 4325376 | tf_op jit(solution)/shard_map/reduce_scatter | solution.py:198
  408.4 124.9 %all-to-all-start.1 = ((bf16[12,100,4,256]{1,2,0,3:T(4,128)(2,1)}), bf16[12,100,4,256]{1,2,0,3:T(4,128)(2,1)}, u32[]{:S(2)}, u32[]{:S(2)}) async-start(bf16[12,100,4,256]{1,2,0,3:T(4,128)(2,1)} %copy.129), calls=%async_computation.1 | async-start | bytes 6291456 | tf_op jit(solution)/shard_map/all_to_all | solution.py:171
  414.1 96.5 %copy-start.55 = (f32[512]{0:T(512)S(1)}, f32[512]{0:T(512)}, u32[]{:S(2)}) copy-start(f32[512]{0:T(512)} %param.37) | copy-start | bytes 6148
  536.0 462.4 %copy-start.1 = (bf16[512,2048]{1,0:T(8,128)(2,1)S(1)}, bf16[512,2048]{1,0:T(8,128)(2,1)}, u32[]{:S(2)}) copy-start(bf16[512,2048]{1,0:T(8,128)(2,1)} %param.34) | copy-start | bytes 6291460
  (43 other events, 149.3 us)
Sparse Core Ops, SparseCore 0:
  331.2 31.3 reduce-scatter.11
  365.4 28.2 reduce-scatter.21
  396.0 28.5 reduce-scatter.23
  427.3 42.3 all-reduce.12
  472.5 135.0 reduce-scatter.15
  613.4 97.9 reduce-scatter.13
  714.2 140.9 reduce-scatter.17
  858.1 140.2 reduce-scatter.19
where the time goes:
time: 1020 us; the launch traced here: 1010 us
  waiting for transfers between devices  542 us (53%)
  matrix products  149 us (15%)
  local copies, waits for them, and re-layouts  126 us (12%)
  blocking collectives  94.2 us (9%)
  other arithmetic  66.5 us (7%)
  between operations  15.4 us (2%)
  starting transfers between devices  11.6 us (1%)
    reduce_scatter x1, waiting for transfers between devices, local(): lax.psum_scatter(grad_fc1, ('win', 'head'), scatter_dimension=0, tiled=True)  144 us
    reduce_scatter x1, waiting for transfers between devices, local(): lax.psum_scatter(grad_fc2, ('win', 'head'), scatter_dimension=0, tiled=True)  143 us
    reduce_scatter x1, waiting for transfers between devices, local(): lax.psum_scatter(grad_qkv, ('win', 'head'), scatter_dimension=0, tiled=True)  104 us
    unnamed x1, blocking collectives  84.3 us
    reduce_scatter x1, waiting for transfers between devices, local(): lax.psum_scatter(grad_proj, ('win', 'head'), scatter_dimension=0, tiled=T...  68.9 us
    all_to_all x1, waiting for transfers between devices, local(): lax.all_to_all(section_rows, 'head', split_axis=0, concat_axis=3, tiled=T...  52.9 us
    reduce_scatter x1, waiting for transfers between devices, local(): lax.psum_scatter(grad_weight.astype(jnp.bfloat16), 'head', scatter_dimens...  29.8 us
    dot_general x1, matrix products, local(): jnp.dot(second_low, fc1_weight, preferred_element_type=jnp.float32)  26.3 us
  transfers between devices with their start and end apart: 10, of which 6 were waited for; matrix products, arithmetic and copies ran while one was open for 10% of the time, Pallas kernels for 0%

commit v1 on v0

v1 whole, which is shorter than its diff:
```python
import functools

import jax
import jax.numpy as jnp
from jax import lax
from jax.experimental import pallas as pl
from jax.experimental.pallas import tpu as pltpu
from jax.sharding import PartitionSpec as P

C2 = 256
DM = 512
HEADS = 16
HD = 32
FF = 2048
WIN = 10
WT = 100
RELS = 361
SPAN = 2 * WIN - 1

QUADS = 4
WIDTH = QUADS * C2
CW = 2
RW = 104
R = CW * RW
JP = 112
LN = 128
GROUPS = 4
PER = 4
LAG = 3
SLOTS = LAG + 1
RB = 16
TILE = 512
EPS = 1e-05
LOG2E = 1.4426950408889634
SCALE = HD ** (-0.5)

MESH = pl.DeviceIdType.MESH
F32 = jnp.float32
BF16 = jnp.bfloat16

O_QB, O_VB, O_PB, O_FC1B, O_FC2B = 0, 512, 1024, 1536, 3584
O_N1G, O_N1B, O_N2G, O_N2B, O_N0G, O_N0B, O_END = 4096, 4608, 5120, 5632, 6144, 7168, 8192


def dot(a, b):
    return lax.dot_general(a, b, (((1,), (0,)), ((), ())), preferred_element_type=F32)


def dot_nt(a, b):
    return lax.dot_general(a, b, (((1,), (1,)), ((), ())), preferred_element_type=F32)


def dot_tn(a, b):
    return lax.dot_general(a, b, (((0,), (0,)), ((), ())), preferred_element_type=F32)


def normalised(v):
    centred = v - jnp.mean(v, axis=-1, keepdims=True)
    inv = lax.rsqrt(jnp.mean(centred * centred, axis=-1, keepdims=True) + EPS)
    return centred * inv, inv


def norm_back(d_out, gain, xhat, inv):
    u = d_out * gain
    mean_u = jnp.mean(u, axis=-1, keepdims=True)
    mean_ux = jnp.mean(u * xhat, axis=-1, keepdims=True)
    return (u - mean_u - xhat * mean_ux) * inv


def fold(v):
    total = v[0:8]
    for r in range(8, v.shape[0], 8):
        total = total + v[r : r + 8]
    return total


def gelu_parts(x):
    z = jnp.abs(x) * 0.7071067811865476
    t = 1.0 / (1.0 + 0.3275911 * z)
    e = jnp.exp2(x * x * (-0.5 * LOG2E))
    poly = ((((1.061405429 * t - 1.453152027) * t + 1.421413741) * t - 0.284496736) * t + 0.254829592) * t
    half = 0.5 * poly * e
    cdf = jnp.where(x < 0, half, 1.0 - half)
    return x * cdf, cdf + x * e * 0.3989422804014327


def split3(v):
    hi = v.astype(BF16)
    rest = v - hi.astype(F32)
    mid = rest.astype(BF16)
    low = (rest - mid.astype(F32)).astype(BF16)
    return hi, mid, low


def offset_of(j):
    return (j // WIN) * SPAN + j % WIN


def kernel(
    n_head, n_chunk, share,
    x_hbm, wp_hbm, n0g, n0b, n1g, n1b, wqkv_hbm, qb, vb, table, wproj_hbm, pb, n2g, n2b,
    wfc1_hbm, fc1b, wfc2_hbm, fc2b, valid, cot_hbm,
    out_ref, sect_hbm, g_fc1, g_fc2, g_qkv, g_proj, g_red, g_small, g_table,
    xv, send_in, rin, rout, wp, wqkv, wproj, wfc1, wfc2, cot,
    nrm, res, fst, qkv, prob, att, stage, sec, sn, dy, wide, act, dh, ffo, dsn, dsec, dpk, d_heads, sums, bias_t, ds_acc,
    in_send, in_recv, out_send, out_recv, x_sem, w_sem, own_sem, sect_sem,
):
    me = lax.axis_index("head")
    lanes = QUADS * share

    def peer(k):
        return lax.rem(me + k, n_head)

    def in_copy(c, k):
        to = peer(k)
        return pltpu.make_async_remote_copy(
            src_ref=send_in.at[c, to], dst_ref=rin.at[c, me], send_sem=in_send.at[c, k], recv_sem=in_recv.at[c, k],
            device_id={"head": to}, device_id_type=MESH,
        )

    def out_copy(c, k):
        to = peer(k)
        return pltpu.make_async_remote_copy(
            src_ref=rin.at[c, to], dst_ref=rout.at[c, me], send_sem=out_send.at[c, k], recv_sem=out_recv.at[c, k],
            device_id={"head": to}, device_id_type=MESH,
        )

    def own_in(c):
        return pltpu.make_async_copy(send_in.at[c, me], rin.at[c, me], own_sem)

    def own_out(c):
        return pltpu.make_async_copy(rin.at[c, me], rout.at[c, me], own_sem)

    def x_copy(c):
        return pltpu.make_async_copy(x_hbm.at[:, c], xv.at[c % 2], x_sem.at[c % 2])

    def sect_copy(c):
        return pltpu.make_async_copy(xv.at[c % 2], sect_hbm.at[:, c], sect_sem.at[c % 2])

    weights = [
        pltpu.make_async_copy(wqkv_hbm, wqkv, w_sem.at[1]),
        pltpu.make_async_copy(wproj_hbm, wproj, w_sem.at[2]),
        pltpu.make_async_copy(wfc1_hbm, wfc1, w_sem.at[3]),
        pltpu.make_async_copy(wfc2_hbm, wfc2, w_sem.at[4]),
        pltpu.make_async_copy(cot_hbm, cot, w_sem.at[5]),
    ]

    for c in range(min(2, n_chunk)):
        x_copy(c).start()
    barrier = pltpu.get_barrier_semaphore()
    for k in range(1, n_head):
        pl.semaphore_signal(barrier, inc=1, device_id={"head": peer(k)}, device_id_type=MESH)
    for q in range(QUADS):
        for s in range(n_head):
            pltpu.make_async_copy(
                wp_hbm.at[q, s], wp.at[pl.ds((s * QUADS + q) * share, share), :], w_sem.at[0]
            ).start()
    for w in weights:
        w.start()

    eye_rows = (
        lax.broadcasted_iota(jnp.int32, (RW, WT), 0) == lax.broadcasted_iota(jnp.int32, (RW, WT), 1)
    ).astype(F32).astype(BF16)
    eye_lanes = (
        lax.broadcasted_iota(jnp.int32, (lanes, lanes), 0) == lax.broadcasted_iota(jnp.int32, (lanes, lanes), 1)
    ).astype(F32).astype(BF16)

    def repack(c):
        x_copy(c).wait()
        for d in range(n_head):
            rows = [dot_nt(eye_rows, xv[c % 2, d, w]) for w in range(CW)]
            send_in[c, d] = jnp.concatenate(rows, axis=0).astype(BF16)

    def send(c):
        for k in range(1, n_head):
            in_copy(c, k).start()
        own_in(c).start()
        own_in(c).wait()

    repack(0)
    pl.semaphore_wait(barrier, n_head - 1)
    send(0)

    def send_rest(c, carry):
        @pl.when(c < n_chunk - 1)
        def _():
            x_copy(c + 1).start()

        repack(c)
        send(c)
        return carry

    lax.fori_loop(1, n_chunk, send_rest, 0)

    def zero(ref):
        def body(r, carry):
            ref[pl.ds(pl.multiple_of(r * 8, 8), 8), :] = jnp.zeros((8, ref.shape[1]), F32)
            return carry
        lax.fori_loop(0, ref.shape[0] // 8, body, 0)

    for ref in (g_fc1, g_fc2, g_qkv, g_proj, g_red, sums):
        zero(ref)
    ds_acc[...] = jnp.zeros_like(ds_acc)

    def zero_heads(c, carry):
        qkv[c] = jnp.zeros(qkv.shape[1:], BF16)
        return carry

    lax.fori_loop(0, SLOTS, zero_heads, 0)
    d_heads[...] = jnp.zeros_like(d_heads)
    bias_t[:, WT:, :] = jnp.full((HEADS, JP - WT, LN), -1e30, F32)

    spot = lax.broadcasted_iota(jnp.int32, (2 * LN, LN), 0)
    token = lax.broadcasted_iota(jnp.int32, (2 * LN, LN), 1)
    token_row = (token * 205) >> 11
    pick = ((spot == token_row * SPAN + token - token_row * WIN) & (token < WT)).astype(F32).astype(BF16)
    for row in range(WIN):
        parts = []
        for col in range(WIN):
            off = offset_of(WT - 1) - offset_of(row * WIN + col)
            parts.append(table[:, off : off + 2 * LN])
        hi, mid, low = split3(jnp.concatenate(parts, axis=0))
        found = (dot(hi, pick) + dot(mid, pick) + dot(low, pick)) * LOG2E
        for col in range(WIN):
            bias_t[:, row * WIN + col, :] = found[col * HEADS : (col + 1) * HEADS]

    pltpu.make_async_copy(wp, wp, w_sem.at[0]).wait()
    for w in weights:
        w.wait()

    lane = lax.broadcasted_iota(jnp.int32, (1, LN), 1)
    masks = [((lane >= h * HD) & (lane < (h + 1) * HD)).astype(F32).astype(BF16) for h in range(PER)]

    def by_head(v):
        return jnp.concatenate([v * m for m in masks], axis=0)

    def merged_rows(c, r):
        return jnp.concatenate([rin[c, s, pl.ds(r, RB), :] for s in range(n_head)], axis=1).astype(F32)

    def padded(v):
        return jnp.concatenate([v, jnp.zeros((JP - RW, v.shape[1]), F32)], axis=0)

    def first_half(c):
        p = lax.rem(c, SLOTS)
        for k in range(1, n_head):
            in_copy_wait = pltpu.make_async_remote_copy(
                src_ref=send_in.at[c, me], dst_ref=rin.at[c, lax.rem(me + n_head - k, n_head)],
                send_sem=in_send.at[c, k], recv_sem=in_recv.at[c, k],
                device_id={"head": peer(k)}, device_id_type=MESH,
            )
            in_copy_wait.wait_recv()
        for r in range(0, R, RB):
            xhat, unused = normalised(merged_rows(c, r))
            nrm[r : r + RB, :] = (xhat * n0g[...] + n0b[...]).astype(BF16)
        res[p] = dot(nrm[...], wp[...])
        for r in range(0, R, RB):
            xhat, unused = normalised(res[p, r : r + RB, :])
            fst[r : r + RB, :] = (xhat * n1g[...] + n1b[...]).astype(BF16)
        for t in range(3):
            part = dot(fst[...], wqkv[:, t * DM : (t + 1) * DM])
            if t == 0:
                part = part + qb[...]
            if t == 2:
                part = part + vb[...]
            for w in range(CW):
                for g in range(GROUPS):
                    piece = part[w * RW : (w + 1) * RW, g * LN : (g + 1) * LN]
                    qkv[p, w, t, g, 0:JP, :] = padded(piece).astype(BF16)

        def attend(w, carry):
            for g in range(GROUPS):
                scores = dot_nt(qkv[p, w, 1, g, 0:JP, :], by_head(qkv[p, w, 0, g]))
                found = []
                for h in range(PER):
                    s = scores[:, h * LN : (h + 1) * LN] * (SCALE * LOG2E) + bias_t[g * PER + h]
                    e = jnp.exp2(s - jnp.max(s, axis=0, keepdims=True))
                    found.append((e * (1.0 / jnp.sum(e, axis=0, keepdims=True))).astype(BF16))
                probs = jnp.concatenate(found, axis=1)
                prob[p, w, g] = probs
                mixed = dot_tn(qkv[p, w, 2, g, 0:JP, :], probs)
                own = jnp.concatenate(
                    [mixed[h * HD : (h + 1) * HD, h * LN : (h + 1) * LN] for h in range(PER)], axis=0
                )
                stage[pl.ds(pl.multiple_of(w * RW, 8), RW), g * LN : (g + 1) * LN] = own.T[0:RW]
            return carry

        lax.fori_loop(0, CW, attend, 0)
        att[p] = stage[:, 0:DM].astype(BF16)
        sec[...] = res[p] + dot(att[p], wproj[...]) + pb[...]
        for r in range(0, R, RB):
            xhat, unused = normalised(sec[r : r + RB, :])
            sn[r : r + RB, :] = (xhat * n2g[...] + n2b[...]).astype(BF16)
        flags = [valid[c * CW + w].astype(F32) for w in range(CW)]
        tail = jnp.zeros((RW - WT, DM), F32)
        pieces = []
        for w in range(CW):
            pieces += [cot[c * CW + w].astype(F32) * flags[w], tail]
        up = jnp.concatenate(pieces, axis=0)
        dy[...] = up.astype(BF16)
        sums[:, O_FC2B : O_FC2B + DM] += fold(up)
        ffo[...] = sec[...] + fc2b[...]
        dsn[...] = jnp.zeros_like(dsn)

        def feed(t, carry):
            cols = pl.ds(pl.multiple_of(t * TILE, TILE), TILE)
            wide[:, 0:TILE] = dot(sn[...], wfc1[:, cols]) + fc1b[:, cols]
            wide[:, TILE : 2 * TILE] = dot_nt(dy[...], wfc2[cols, :])
            total = jnp.zeros((8, TILE), F32)
            for r in range(0, R, RB):
                value, slope = gelu_parts(wide[r : r + RB, 0:TILE])
                act[r : r + RB, :] = value.astype(BF16)
                low = (wide[r : r + RB, TILE : 2 * TILE] * slope).astype(BF16)
                dh[r : r + RB, :] = low
                total = total + fold(low.astype(F32))
            sums[:, pl.ds(pl.multiple_of(O_FC1B + t * TILE, TILE), TILE)] += total
            ffo[...] += dot(act[...], wfc2[cols, :])
            dsn[...] += dot_nt(dh[...], wfc1[:, cols])
            g_fc2[cols, :] += dot_tn(act[...], dy[...])
            g_fc1[:, cols] += dot_tn(sn[...], dh[...])
            return carry

        lax.fori_loop(0, FF // TILE, feed, 0)
        for w in range(CW):
            out_ref[c * CW + w] = (ffo[w * RW : w * RW + WT, :] * flags[w]).astype(BF16)
        sum_g = jnp.zeros((8, DM), F32)
        sum_b = jnp.zeros((8, DM), F32)
        for r in range(0, R, RB):
            xhat, inv = normalised(sec[r : r + RB, :])
            d_out = dsn[r : r + RB, :]
            sum_g = sum_g + fold(d_out * xhat)
            sum_b = sum_b + fold(d_out)
            dsec[p, r : r + RB, :] = norm_back(d_out, n2g[...], xhat, inv) + dy[r : r + RB, :].astype(F32)
        sums[:, O_N2G : O_N2G + DM] += sum_g
        sums[:, O_N2B : O_N2B + DM] += sum_b

    def second_half(c):
        p = lax.rem(c, SLOTS)
        low = dsec[p].astype(BF16)
        sums[:, O_PB : O_PB + DM] += fold(low.astype(F32))
        dy[...] = low
        g_proj[...] += dot_tn(att[p], dy[...])
        back = dot_nt(dy[...], wproj[...])
        for w in range(CW):
            for g in range(GROUPS):
                piece = back[w * RW : (w + 1) * RW, g * LN : (g + 1) * LN]
                d_heads[w, g, 0:JP, :] = padded(piece).astype(BF16)

        def attend(w, carry):
            for g in range(GROUPS):
                d_out = by_head(d_heads[w, g])
                q_all = by_head(qkv[p, w, 0, g])
                d_probs = dot_nt(qkv[p, w, 2, g, 0:JP, :], d_out)
                raw = []
                for h in range(PER):
                    pr = prob[p, w, g, :, h * LN : (h + 1) * LN].astype(F32)
                    dp = d_probs[:, h * LN : (h + 1) * LN]
                    pd = pr * dp
                    d_s = pd - pr * jnp.sum(pd, axis=0, keepdims=True)
                    ds_acc[g * PER + h] += d_s
                    raw.append((d_s * SCALE).astype(BF16))
                d_raw = jnp.concatenate(raw, axis=1)
                rows = pl.ds(pl.multiple_of(w * RW, 8), RW)
                d_v = dot(prob[p, w, g], d_out)
                d_k = dot(d_raw, q_all)
                mixed = dot_tn(qkv[p, w, 1, g, 0:JP, :], d_raw)
                own = jnp.concatenate(
                    [mixed[h * HD : (h + 1) * HD, h * LN : (h + 1) * LN] for h in range(PER)], axis=0
                )
                stage[rows, g * LN : (g + 1) * LN] = own.T[0:RW]
                stage[rows, DM + g * LN : DM + (g + 1) * LN] = d_k[0:RW]
                stage[rows, 2 * DM + g * LN : 2 * DM + (g + 1) * LN] = d_v[0:RW]
            return carry

        lax.fori_loop(0, CW, attend, 0)
        sum_g = jnp.zeros((8, DM), F32)
        sum_b = jnp.zeros((8, DM), F32)
        sum_q = jnp.zeros((8, DM), F32)
        sum_v = jnp.zeros((8, DM), F32)
        for r in range(0, R, RB):
            low = stage[r : r + RB, :].astype(BF16)
            dpk[r : r + RB, :] = low
            sum_q = sum_q + fold(low[:, 0:DM].astype(F32))
            sum_v = sum_v + fold(low[:, 2 * DM :].astype(F32))
        sums[:, O_QB : O_QB + DM] += sum_q
        sums[:, O_VB : O_VB + DM] += sum_v
        dsn[...] = dot_nt(dpk[...], wqkv[...])
        for r in range(0, R, RB):
            xhat, inv = normalised(res[p, r : r + RB, :])
            fst[r : r + RB, :] = (xhat * n1g[...] + n1b[...]).astype(BF16)
            d_out = dsn[r : r + RB, :]
            sum_g = sum_g + fold(d_out * xhat)
            sum_b = sum_b + fold(d_out)
            d_res = norm_back(d_out, n1g[...], xhat, inv) + dsec[p, r : r + RB, :]
            sn[r : r + RB, :] = d_res.astype(BF16)
        sums[:, O_N1G : O_N1G + DM] += sum_g
        sums[:, O_N1B : O_N1B + DM] += sum_b
        wide[...] = dot_nt(sn[...], wp[...])
        sum_g = jnp.zeros((8, WIDTH), F32)
        sum_b = jnp.zeros((8, WIDTH), F32)
        for r in range(0, R, RB):
            xhat, inv = normalised(merged_rows(c, r))
            nrm[r : r + RB, :] = (xhat * n0g[...] + n0b[...]).astype(BF16)
            d_out = wide[r : r + RB, :]
            sum_g = sum_g + fold(d_out * xhat)
            sum_b = sum_b + fold(d_out)
            low = norm_back(d_out, n0g[...], xhat, inv).astype(BF16)
            for s in range(n_head):
                rin[c, s, r : r + RB, :] = low[:, s * lanes : (s + 1) * lanes]
        sums[:, O_N0G : O_N0G + WIDTH] += sum_g
        sums[:, O_N0B : O_N0B + WIDTH] += sum_b
        for k in range(1, n_head):
            out_copy(c, k).start()
        own_out(c).start()
        g_qkv[...] += dot_tn(fst[...], dpk[...])
        g_red[...] += dot_tn(nrm[...], sn[...])
        own_out(c).wait()

    def step(s, carry):
        @pl.when(s < n_chunk)
        def _():
            first_half(s)

        @pl.when(s >= LAG)
        def _():
            second_half(s - LAG)

        return carry

    lax.fori_loop(0, n_chunk + LAG, step, 0)

    def unpack(c, carry):
        for k in range(1, n_head):
            pltpu.make_async_remote_copy(
                src_ref=rin.at[c, me], dst_ref=rout.at[c, lax.rem(me + n_head - k, n_head)],
                send_sem=out_send.at[c, k], recv_sem=out_recv.at[c, k],
                device_id={"head": peer(k)}, device_id_type=MESH,
            ).wait_recv()

        @pl.when(c >= 2)
        def _():
            sect_copy(c - 2).wait()

        for s in range(n_head):
            turned = dot_nt(eye_lanes, rout[c, s])
            for w in range(CW):
                xv[c % 2, s, w] = turned[:, w * RW : w * RW + WT].astype(BF16)
        sect_copy(c).start()
        return carry

    lax.fori_loop(0, n_chunk, unpack, 0)
    for c in range(max(0, n_chunk - 2), n_chunk):
        sect_copy(c).wait()

    g_small[...] = jnp.sum(sums[...], axis=0, keepdims=True)
    g_table[...] = jnp.zeros_like(g_table)
    for row in range(WIN):
        spread = jnp.zeros((WIN * HEADS, 2 * LN), F32)
        whole = jnp.concatenate([ds_acc[:, row * WIN + col, :] for col in range(WIN)], axis=0)
        for part in split3(whole):
            spread = spread + dot_nt(part, pick)
        for col in range(WIN):
            off = offset_of(WT - 1) - offset_of(row * WIN + col)
            g_table[:, off : off + 2 * LN] += spread[col * HEADS : (col + 1) * HEADS]

    def drain(c, carry):
        for k in range(1, n_head):
            in_copy(c, k).wait_send()
            out_copy(c, k).wait_send()
        return carry

    lax.fori_loop(0, n_chunk, drain, 0)


def run_kernel(n_head, n_chunk, share, args):
    lanes = QUADS * share
    any_, vmem = pl.BlockSpec(memory_space=pl.ANY), pl.BlockSpec(memory_space=pltpu.VMEM)
    smem = pl.BlockSpec(memory_space=pltpu.SMEM)
    windows = n_chunk * CW
    in_specs = [
        any_, any_, vmem, vmem, vmem, vmem, any_, vmem, vmem, vmem, any_, vmem, vmem, vmem,
        any_, vmem, any_, vmem, smem, any_,
    ]
    out_shape = [
        jax.ShapeDtypeStruct((windows, WT, DM), BF16),
        jax.ShapeDtypeStruct((n_head, n_chunk, CW, lanes, WT), BF16),
        jax.ShapeDtypeStruct((DM, FF), F32),
        jax.ShapeDtypeStruct((FF, DM), F32),
        jax.ShapeDtypeStruct((DM, 3 * DM), F32),
        jax.ShapeDtypeStruct((DM, DM), F32),
        jax.ShapeDtypeStruct((WIDTH, DM), F32),
        jax.ShapeDtypeStruct((1, O_END), F32),
        jax.ShapeDtypeStruct((HEADS, 4 * LN), F32),
    ]
    out_specs = [vmem, any_] + [vmem] * 7
    dma = pltpu.SemaphoreType.DMA
    scratch = [
        pltpu.VMEM((2, n_head, CW, lanes, WT), BF16),
        pltpu.VMEM((n_chunk, n_head, R, lanes), BF16),
        pltpu.VMEM((n_chunk, n_head, R, lanes), BF16),
        pltpu.VMEM((n_chunk, n_head, R, lanes), BF16),
        pltpu.VMEM((WIDTH, DM), BF16),
        pltpu.VMEM((DM, 3 * DM), BF16),
        pltpu.VMEM((DM, DM), BF16),
        pltpu.VMEM((DM, FF), BF16),
        pltpu.VMEM((FF, DM), BF16),
        pltpu.VMEM((windows, WT, DM), BF16),
        pltpu.VMEM((R, WIDTH), BF16),
        pltpu.VMEM((SLOTS, R, DM), F32),
        pltpu.VMEM((R, DM), BF16),
        pltpu.VMEM((SLOTS, CW, 3, GROUPS, LN, LN), BF16),
        pltpu.VMEM((SLOTS, CW, GROUPS, JP, PER * LN), BF16),
        pltpu.VMEM((SLOTS, R, DM), BF16),
        pltpu.VMEM((R, 3 * DM), F32),
        pltpu.VMEM((R, DM), F32),
        pltpu.VMEM((R, DM), BF16),
        pltpu.VMEM((R, DM), BF16),
        pltpu.VMEM((R, WIDTH), F32),
        pltpu.VMEM((R, TILE), BF16),
        pltpu.VMEM((R, TILE), BF16),
        pltpu.VMEM((R, DM), F32),
        pltpu.VMEM((R, DM), F32),
        pltpu.VMEM((SLOTS, R, DM), F32),
        pltpu.VMEM((R, 3 * DM), BF16),
        pltpu.VMEM((CW, GROUPS, LN, LN), BF16),
        pltpu.VMEM((8, O_END), F32),
        pltpu.VMEM((HEADS, JP, LN), F32),
        pltpu.VMEM((HEADS, JP, LN), F32),
        dma((n_chunk, n_head)), dma((n_chunk, n_head)), dma((n_chunk, n_head)), dma((n_chunk, n_head)),
        dma((2,)), dma((6,)), dma, dma((2,)),
    ]
    return pl.pallas_call(
        functools.partial(kernel, n_head, n_chunk, share),
        out_shape=out_shape, in_specs=in_specs, out_specs=out_specs, scratch_shapes=scratch,
        compiler_params=pltpu.CompilerParams(
            collective_id=0, has_side_effects=True, vmem_limit_bytes=63 * 1024 * 1024
        ),
        cost_estimate=pl.CostEstimate(flops=27 * 10**9, bytes_accessed=30 * 10**6, transcendentals=10**7),
    )(*args)


def local(
    n_head, section_rows, reduce_weight, norm0_gain, norm0_bias, norm1_gain, norm1_bias, qkv_weight, q_bias, v_bias,
    rel_table, proj_weight, proj_bias, norm2_gain, norm2_bias, fc1_weight, fc1_bias, fc2_weight, fc2_bias,
    window_valid, cotangent,
):
    group_windows, tokens, quads, share = section_rows.shape
    windows = cotangent.shape[0]
    n_chunk = windows // CW
    lanes = quads * share
    rows = section_rows.transpose(0, 2, 3, 1).reshape(n_head, n_chunk, CW, lanes, tokens)

    def by_source(v):
        return v.reshape(quads, n_head, share).transpose(1, 0, 2).reshape(1, WIDTH)

    def row(v):
        return v.reshape(1, -1)

    args = (
        rows, reduce_weight.reshape(quads, n_head, share, DM), by_source(norm0_gain), by_source(norm0_bias),
        row(norm1_gain), row(norm1_bias), qkv_weight, row(q_bias), row(v_bias),
        jnp.pad(rel_table, ((0, 0), (0, 4 * LN - RELS))), proj_weight, row(proj_bias), row(norm2_gain), row(norm2_bias),
        fc1_weight, row(fc1_bias), fc2_weight, row(fc2_bias), window_valid, cotangent,
    )
    block_out, section, fc1, fc2, qkv, proj, red, small, table = run_kernel(n_head, n_chunk, share, args)
    section_grad = section.reshape(group_windows, quads, share, tokens).transpose(0, 3, 1, 2)
    both = ("win", "head")

    def scattered(v):
        return lax.psum_scatter(v.astype(BF16), both, scatter_dimension=0, tiled=True).astype(F32)

    mine = lax.psum_scatter(red.astype(BF16), "head", scatter_dimension=0, tiled=True)
    reduce_grad = lax.psum(mine, "win").astype(F32).reshape(quads, share, DM)
    vectors, table_grad = lax.psum((small[0], table), both)
    table_grad = table_grad[:, :RELS]
    at = lax.axis_index("win") * n_head + lax.axis_index("head")
    devices = lax.axis_size("win") * n_head

    def part(start, length):
        size = length // devices
        return lax.dynamic_slice_in_dim(vectors, start + at * size, size)

    def part0(start):
        return lax.dynamic_slice_in_dim(vectors, start + lax.axis_index("head") * lanes, lanes).reshape(quads, share)

    return (
        block_out, section_grad, reduce_grad, part0(O_N0G), part0(O_N0B), part(O_N1G, DM), part(O_N1B, DM),
        scattered(qkv), part(O_QB, DM), part(O_VB, DM), table_grad, scattered(proj), part(O_PB, DM),
        part(O_N2G, DM), part(O_N2B, DM), scattered(fc1), part(O_FC1B, FF), scattered(fc2), part(O_FC2B, DM),
    )

def solution(mesh):
    in_specs = (
        P("win", None, None, "head"),
        P(),
        P(),
        P(),
        P(),
        P(),
        P(),
        P(),
        P(),
        P(),
        P(),
        P(),
        P(),
        P(),
        P(),
        P(),
        P(),
        P(),
        P(("win", "head")),
        P(("win", "head"), None, None),
    )
    out_specs = (
        P(("win", "head"), None, None),
        P("win", None, None, "head"),
        P(None, "head", None),
        P(None, "head"),
        P(None, "head"),
        P(("win", "head")),
        P(("win", "head")),
        P(("win", "head"), None),
        P(("win", "head")),
        P(("win", "head")),
        P(),
        P(("win", "head"), None),
        P(("win", "head")),
        P(("win", "head")),
        P(("win", "head")),
        P(("win", "head"), None),
        P(("win", "head")),
        P(("win", "head"), None),
        P(("win", "head")),
    )
    return jax.shard_map(
        functools.partial(local, mesh.shape["head"]), mesh=mesh, in_specs=in_specs, out_specs=out_specs, check_vma=False)
```

time: 1020 us -> 716 us (0.70); the launches traced: 1010 us -> 716 us
  matrix products: 149 us -> 0 us
  Pallas kernels: 0 us -> 142 us
  local copies, waits for them, and re-layouts: 126 us -> 14.5 us
  blocking collectives: 94.2 us -> 0 us
  other arithmetic: 66.5 us -> 21.5 us
  waiting for transfers between devices: 542 us -> 522 us
  starting transfers between devices: 11.6 us -> 0.29 us
    dot_general x23 -> x0, matrix products: 149 us -> none  [the longest x1 26.3 us: local(): jnp.dot(second_low, fc1_weight, preferred_element_type=jnp.float32)]
    pallas_call x0 -> x1, Pallas kernels: none -> 142 us  [run_kernel(): pl.pallas_call(functools.partial(kernel, n_head, n_chunk, share), out_sha...]
    psum x1 -> x2, waiting for transfers between devices: 0.01 us -> 85.8 us  [the longest x1 85.8 us: local(): vectors, table_grad = lax.psum((small[0], table), both)]
    unnamed x1 -> x0, blocking collectives: 84.3 us -> none
    reduce_scatter x5, waiting for transfers between devices: 489 us -> 436 us  [the longest x4 402 us: scattered(): lax.psum_scatter(v.astype(BF16), both, scatter_dimension=0, tiled=True)]
    all_to_all x2 -> x0, waiting for transfers between devices: 52.9 us -> none  [the longest x1 52.9 us: local(): lax.all_to_all(section_rows, 'head', split_axis=0, concat_axis=3, tiled=T...]
    convert_element_type x13 -> x0, local copies, waits for them, and re-layouts: 46.2 us -> none  [the longest x3 23.1 us: local(): merged = gathered.astype(jnp.float32).reshape(rows, width)]
    reshape x12 -> x8, local copies, waits for them, and re-layouts: 49.8 us -> 4.23 us  [the longest x6 2.91 us: by_source(): return v.reshape(quads, n_head, share).transpose(1, 0, 2).reshape(1, WIDTH)]
  transfers between devices with their start and end apart: 10 -> 7, of which waited for: 6 -> 6; matrix products, arithmetic and copies ran while one was open for 10% -> 3% of each run, Pallas kernels for 0% -> 0%
where the time goes in v1:
time: 716 us
  waiting for transfers between devices  522 us (73%)
  Pallas kernels  142 us (20%)
  other arithmetic  21.5 us (3%)
  between operations  15.3 us (2%)
  local copies, waits for them, and re-layouts  14.5 us (2%)
    reduce_scatter x4, waiting for transfers between devices, scattered(): lax.psum_scatter(v.astype(BF16), both, scatter_dimension=0, tiled=True)  402 us
    pallas_call x1, Pallas kernels, run_kernel(): pl.pallas_call(functools.partial(kernel, n_head, n_chunk, share), out_sha...  142 us
    psum x1, waiting for transfers between devices, local(): vectors, table_grad = lax.psum((small[0], table), both)  85.8 us
    reduce_scatter x1, waiting for transfers between devices, local(): lax.psum_scatter(red.astype(BF16), 'head', scatter_dimension=0, tiled=True)  33.7 us
  transfers between devices with their start and end apart: 7, of which 6 were waited for; matrix products, arithmetic and copies ran while one was open for 3% of the time, Pallas kernels for 0%

profile of v1, /device:TPU:0, one launch (start us, length us, event | category | flops | bytes accessed | tf_op | source)
XLA Modules:
  0.0 715.6 jit_solution(15387696533267847090)
XLA Ops:
  8.1 0.8 reshape.100
  11.0 1.4 pad.4.table
  12.3 142.0 %shard_map.339 = (bf16[12,100,512]{2,1,0:T(8,128)(2,1)}, bf16[8,6,2,128,100]{4,3,2,1,0:T(8,128)(2,1)}, f32[512,2048]{1,0:T(8,128)}, f32[2048,512]{1,0:T(8,128)},...) custom-call(bf16[8,6,2,128,100]{4,3,2,1,0:T(8,128)(2,1)} %bitcast.29, ...), custom_call_target="tpu_custom_call" | custom-call | flops 27000000512 | bytes 30000000 | tf_op jit(solution)/shard_map/pallas_call | solution.py:531
  154.4 2.7 convert_element_type.30
  157.7 2.4 convert_element_type.33
  160.2 1.4 convert_element_type.31
  161.7 33.7 %reduce-scatter.6.cloned.1.call-done = bf16[128,512]{1,0:T(8,128)(2,1)} async-done(((bf16[1024,512]{1,0:T(8,128)(2,1)}), bf16[128,512]{1,0:T(8,128)(2,1)}) %reduce-scatter.6.cloned.1.call-update) | async-done | bytes 131088 | tf_op jit(solution)/shard_map/reduce_scatter | solution.py:571
  195.4 3.8 convert_element_type.35
  199.4 3.8 convert_element_type.37
  203.2 85.8 %all-reduce.7.cloned.1.call-done = (f32[8192]{0:T(1024)}, f32[16,512]{1,0:T(8,128)}) async-done(((f32[8192]{0:T(1024)}, f32[16,512]{1,0:T(8,128)}), (f32[8192]{0:T(1024)}, f32[16,512]{1,0:T(8,128)})) %all-reduce.7.cloned.1.call-update) | async-done | bytes 65552 | tf_op jit(solution)/shard_map/psum | solution.py:573
  291.1 1.3 dynamic_slice.42
  292.3 1.3 slice.4
  293.7 1.4 fusion
  295.1 34.9 %reduce-scatter.10.cloned.1.call-done = bf16[16,512]{1,0:T(8,128)(2,1)} async-done(((bf16[512,512]{1,0:T(8,128)(2,1)}), bf16[16,512]{1,0:T(8,128)(2,1)}) %reduce-scatter.10.cloned.1.call-update) | async-done | bytes 16400 | tf_op jit(solution)/shard_map/reduce_scatter | solution.py:569
  330.0 1.3 convert_element_type.34
  331.3 97.2 %reduce-scatter.8.cloned.1.call-done = bf16[16,1536]{1,0:T(8,128)(2,1)} async-done(((bf16[512,1536]{1,0:T(8,128)(2,1)}), bf16[16,1536]{1,0:T(8,128)(2,1)}) %reduce-scatter.8.cloned.1.call-update) | async-done | bytes 49168 | tf_op jit(solution)/shard_map/reduce_scatter | solution.py:569
  428.5 1.4 convert_element_type.32
  429.9 1.6 reshape.115
  431.6 135.8 %reduce-scatter.12.cloned.1.call-done = bf16[16,2048]{1,0:T(8,128)(2,1)} async-done(((bf16[512,2048]{1,0:T(8,128)(2,1)}), bf16[16,2048]{1,0:T(8,128)(2,1)}) %reduce-scatter.12.cloned.1.call-update) | async-done | bytes 65552 | tf_op jit(solution)/shard_map/reduce_scatter | solution.py:569
  567.3 1.5 convert_element_type.36
  568.8 134.0 %reduce-scatter.14.cloned.1.call-done = bf16[64,512]{1,0:T(8,128)(2,1)} async-done(((bf16[2048,512]{1,0:T(8,128)(2,1)}), bf16[64,512]{1,0:T(8,128)(2,1)}) %reduce-scatter.14.cloned.1.call-update) | async-done | bytes 65552 | tf_op jit(solution)/shard_map/reduce_scatter | solution.py:569
  702.9 1.5 convert_element_type.38
  704.4 2.4 copy.50
  706.8 1.7 copy.51
  (27 shorter events, 5.1 us)
Async XLA Ops:
  8.0 187.3 %reduce-scatter.6.cloned.1.call-start = ((), (), s32[]{:S(2)}) async-start(), calls=%async_computation.5 | async-start | bytes 1179648 | tf_op jit(solution)/shard_map/reduce_scatter | solution.py:571
  157.1 3.1 copy-start.1
  157.1 131.9 %all-reduce.7.cloned.1.call-start = ((), (), s32[]{:S(2)}) async-start(), calls=%async_computation.11 | async-start | bytes 131072 | tf_op jit(solution)/shard_map/psum | solution.py:573
  157.7 172.3 %reduce-scatter.10.cloned.1.call-start = ((), (), s32[]{:S(2)}) async-start(), calls=%async_computation.8 | async-start | bytes 540672 | tf_op jit(solution)/shard_map/reduce_scatter | solution.py:569
  160.1 268.4 %reduce-scatter.8.cloned.1.call-start = ((), (), s32[]{:S(2)}) async-start(), calls=%async_computation.7 | async-start | bytes 1622016 | tf_op jit(solution)/shard_map/reduce_scatter | solution.py:569
  161.6 268.3 %all-reduce.5.cloned.1.call-start = ((), (), s32[]{:S(2)}) async-start(), calls=%async_computation.6 | async-start | bytes 262144 | tf_op jit(solution)/shard_map/psum | solution.py:572
  195.4 371.9 %reduce-scatter.12.cloned.1.call-start = ((), (), s32[]{:S(2)}) async-start(), calls=%async_computation.9 | async-start | bytes 2162688 | tf_op jit(solution)/shard_map/reduce_scatter | solution.py:569
  199.3 503.5 %reduce-scatter.14.cloned.1.call-start = ((), (), s32[]{:S(2)}) async-start(), calls=%async_computation.10 | async-start | bytes 2162688 | tf_op jit(solution)/shard_map/reduce_scatter | solution.py:569
  203.2 503.6 %copy-start = (bf16[8,6,2,128,100]{4,3,2,1,0:T(8,128)(2,1)S(1)}, bf16[8,6,2,128,100]{4,3,2,1,0:T(8,128)(2,1)}, u32[]{:S(2)}) copy-start(bf16[8,6,2,128,100]{4,3,2,1,0:T(8,128)(2,1)} %get-tuple-element.29) | copy-start | bytes 7372804
Sparse Core Ops, SparseCore 0:
  157.2 38.0 reduce-scatter.5
  197.7 132.2 reduce-scatter.9
  335.2 93.2 reduce-scatter.7
  431.2 136.1 reduce-scatter.11
  569.5 133.2 reduce-scatter.13
Sparse Core Ops, SparseCore 1:
  163.3 125.7 all-reduce.6
  291.7 42.3 all-reduce.4

commit v2 on v1

--- a/solution.py
+++ b/solution.py
@@ -28,6 +28,7 @@
 PER = 4
 LAG = 3
 SLOTS = LAG + 1
+UNPACK_LAG = LAG + 2
 RB = 16
 TILE = 512
 EPS = 1e-05
@@ -40,6 +41,9 @@
 
 O_QB, O_VB, O_PB, O_FC1B, O_FC2B = 0, 512, 1024, 1536, 3584
 O_N1G, O_N1B, O_N2G, O_N2B, O_N0G, O_N0B, O_END = 4096, 4608, 5120, 5632, 6144, 7168, 8192
+
+
+MATRICES = ((DM, FF), (FF, DM), (DM, 3 * DM), (DM, DM), (WIDTH, DM))
 
 
 def dot(a, b):
@@ -97,19 +101,195 @@
 
 
 def kernel(
-    n_head, n_chunk, share,
+    n_head, n_win, n_chunk, share,
     x_hbm, wp_hbm, n0g, n0b, n1g, n1b, wqkv_hbm, qb, vb, table, wproj_hbm, pb, n2g, n2b,
     wfc1_hbm, fc1b, wfc2_hbm, fc2b, valid, cot_hbm,
-    out_ref, sect_hbm, g_fc1, g_fc2, g_qkv, g_proj, g_red, g_small, g_table,
-    xv, send_in, rin, rout, wp, wqkv, wproj, wfc1, wfc2, cot,
+    *refs,
+):
+    if n_win is None:
+        (out_ref, sect_hbm, g_fc1, g_fc2, g_qkv, g_proj, g_red, g_small), refs = refs[:8], refs[8:]
+    else:
+        (out_ref, sect_hbm, o_fc1, o_fc2, o_qkv, o_proj, o_red, g_small), refs = refs[:8], refs[8:]
+        (g_fc1, g_fc2, g_qkv, g_proj, g_red), refs = refs[:5], refs[5:]
+        first_in, refs = refs[:5], refs[5:]
+        plane_in, refs = refs[:5], refs[5:]
+        near_in, refs = refs[:5], refs[5:]
+        far_in, refs = refs[:5], refs[5:]
+        (gather_in, small_in, sum_send, sum_recv), refs = refs[:4], refs[4:]
+    (xv, send_in, rin, rout, wp, wqkv, wproj, wfc1, wfc2, cot,
     nrm, res, fst, qkv, prob, att, stage, sec, sn, dy, wide, act, dh, ffo, dsn, dsec, dpk, d_heads, sums, bias_t, ds_acc,
-    in_send, in_recv, out_send, out_recv, x_sem, w_sem, own_sem, sect_sem,
-):
+    in_send, in_recv, out_send, out_recv, x_sem, w_sem, own_sem, sect_sem) = refs
     me = lax.axis_index("head")
     lanes = QUADS * share
 
     def peer(k):
         return lax.rem(me + k, n_head)
+
+    if n_win is not None:
+        my_win = lax.axis_index("win")
+        core, my_z = lax.rem(me, 2), me // 2
+        n_z = n_head // 2
+        sibling = me + 1 - 2 * core
+        near_z = my_z + 1 - 2 * lax.rem(my_z, 2)
+        far_z = my_z + 2 - 4 * (my_z // 2)
+
+        def win_peer(k):
+            return lax.rem(my_win + k, n_win)
+
+        class Scatter:
+            def __init__(self, spot, total, hold, out, by_head=False):
+                self.spot, self.total, self.hold, self.out = spot, total, hold, out
+                self.rows = total.shape[0] // (n_win * n_head)
+                self.cols = total.shape[1]
+                self.by_head = by_head
+                half = total.shape[0] // 2
+                self.at_plane = half
+                self.at_near = half + (n_win - 1) * n_z * self.rows
+                self.at_far = self.at_near + (n_z // 2) * self.rows
+
+            def block(self, w, z, c):
+                head = z * 2 + c
+                spot = head * n_win + w if self.by_head else w * n_head + head
+                return pl.ds(pl.multiple_of(spot * self.rows, 16), self.rows)
+
+            def span(self, start, count=1):
+                return pl.ds(pl.multiple_of(start, 16), count * self.rows)
+
+            def copy(self, j, source, target, to):
+                return pltpu.make_async_remote_copy(
+                    src_ref=source, dst_ref=target, send_sem=sum_send.at[self.spot, j], recv_sem=sum_recv.at[self.spot, j],
+                    device_id=to, device_id_type=MESH,
+                )
+
+            def pair_copy(self):
+                return self.copy(
+                    0, self.hold.at[pl.ds(0, self.at_plane), :], first_in[self.spot], {"head": sibling}
+                )
+
+            def plane_copy(self, k):
+                source = self.hold.at[self.span(self.at_plane + (k - 1) * n_z * self.rows, n_z), :]
+                return self.copy(k, source, plane_in[self.spot].at[k - 1], {"win": win_peer(k)})
+
+            def near_copy(self):
+                source = self.hold.at[self.span(self.at_near, n_z // 2), :]
+                return self.copy(n_win, source, near_in[self.spot], {"head": near_z * 2 + core})
+
+            def far_copy(self):
+                source = self.hold.at[self.span(self.at_far), :]
+                return self.copy(n_win + 1, source, far_in[self.spot], {"head": far_z * 2 + core})
+
+            def start_pair(self):
+                def body(i, carry):
+                    w, z = i // n_z, lax.rem(i, n_z)
+                    self.hold[self.span(i * self.rows), :] = self.total[self.block(w, z, 1 - core), :].astype(BF16)
+                    return carry
+
+                lax.fori_loop(0, n_win * n_z, body, 0)
+                self.pair_copy().start()
+
+            def start_plane(self):
+                self.pair_copy().wait_recv()
+                for k in range(1, n_win + 1):
+                    w = lax.rem(my_win + k, n_win)
+
+                    def body(z, carry):
+                        mine = self.block(w, z, core)
+                        value = self.total[mine, :] + first_in[self.spot][
+                            self.span((w * n_z + z) * self.rows), :
+                        ].astype(F32)
+                        if k == n_win:
+                            self.total[mine, :] = value
+                        else:
+                            at = self.at_plane + ((k - 1) * n_z + z) * self.rows
+                            self.hold[self.span(at), :] = value.astype(BF16)
+                        return carry
+
+                    lax.fori_loop(0, n_z, body, 0)
+                    if k < n_win:
+                        self.plane_copy(k).start()
+
+            def start_near(self):
+                for k in range(1, n_win):
+                    self.plane_copy(k).wait_recv()
+
+                def both(z):
+                    value = self.total[self.block(my_win, z, core), :]
+                    for k in range(1, n_win):
+                        value = value + plane_in[self.spot][k - 1, self.span(z * self.rows), :].astype(F32)
+                    return value
+
+                for j in range(n_z // 2):
+                    sent = both(j * 2 + lax.rem(near_z, 2))
+                    self.hold[self.span(self.at_near + j * self.rows), :] = sent.astype(BF16)
+                self.near_copy().start()
+                for j in range(n_z // 2):
+                    z = j * 2 + lax.rem(my_z, 2)
+                    self.total[self.block(my_win, z, core), :] = both(z)
+
+            def after_near(self, j):
+                kept = self.total[self.block(my_win, j * 2 + lax.rem(my_z, 2), core), :]
+                return kept + near_in[self.spot][self.span(j * self.rows), :].astype(F32)
+
+            def start_far(self):
+                self.near_copy().wait_recv()
+                self.hold[self.span(self.at_far), :] = self.after_near(far_z // 2).astype(BF16)
+                self.far_copy().start()
+
+            def finish(self):
+                self.far_copy().wait_recv()
+                value = self.after_near(my_z // 2) + far_in[self.spot][...].astype(F32)
+                if not self.by_head:
+                    self.out[...] = value
+                    return
+                gather_in[my_win] = value.astype(BF16)
+                for k in range(1, n_win):
+                    self.gather_copy(k).start()
+
+            def gather_copy(self, k):
+                return self.copy(
+                    n_win + 1 + k, gather_in.at[my_win], gather_in.at[my_win], {"win": win_peer(k)}
+                )
+
+            def finish_gather(self):
+                for k in range(1, n_win):
+                    source = lax.rem(my_win + n_win - k, n_win)
+                    self.copy(
+                        n_win + 1 + k, gather_in.at[my_win], gather_in.at[source], {"win": win_peer(k)}
+                    ).wait_recv()
+                for w in range(n_win):
+                    self.out[w * self.rows : (w + 1) * self.rows, :] = gather_in[w].astype(F32)
+
+            def drain(self):
+                self.pair_copy().wait_send()
+                for k in range(1, n_win):
+                    self.plane_copy(k).wait_send()
+                    if self.by_head:
+                        self.gather_copy(k).wait_send()
+                self.near_copy().wait_send()
+                self.far_copy().wait_send()
+
+        feeds = [Scatter(0, g_fc1, wfc1, o_fc1), Scatter(1, g_fc2, wfc2, o_fc2)]
+        others = [Scatter(2, g_qkv, wqkv, o_qkv), Scatter(3, g_proj, wproj, o_proj), Scatter(4, g_red, wp, o_red, True)]
+
+        def small_copy(j, source, target, to):
+            return pltpu.make_async_remote_copy(
+                src_ref=small_in.at[source], dst_ref=small_in.at[target], send_sem=sum_send.at[5, j],
+                recv_sem=sum_recv.at[5, j], device_id=to, device_id_type=MESH,
+            )
+
+        at_pair, at_plane, at_near, at_far = 0, 2, 2 + n_win, 4 + n_win
+
+        def small_pair():
+            return small_copy(0, at_pair, at_pair + 1, {"head": sibling})
+
+        def small_plane(k, target=None):
+            return small_copy(k, at_plane + my_win, at_plane + (my_win if target is None else target), {"win": win_peer(k)})
+
+        def small_near():
+            return small_copy(n_win, at_near, at_near + 1, {"head": near_z * 2 + core})
+
+        def small_far():
+            return small_copy(n_win + 1, at_far, at_far + 1, {"head": far_z * 2 + core})
 
     def in_copy(c, k):
         to = peer(k)
@@ -150,6 +330,9 @@
     barrier = pltpu.get_barrier_semaphore()
     for k in range(1, n_head):
         pl.semaphore_signal(barrier, inc=1, device_id={"head": peer(k)}, device_id_type=MESH)
+    if n_win is not None:
+        for k in range(1, n_win):
+            pl.semaphore_signal(barrier, inc=1, device_id={"win": win_peer(k)}, device_id_type=MESH)
     for q in range(QUADS):
         for s in range(n_head):
             pltpu.make_async_copy(
@@ -178,7 +361,7 @@
         own_in(c).wait()
 
     repack(0)
-    pl.semaphore_wait(barrier, n_head - 1)
+    pl.semaphore_wait(barrier, n_head - 1 + (0 if n_win is None else n_win - 1))
     send(0)
 
     def send_rest(c, carry):
@@ -415,20 +598,7 @@
         g_red[...] += dot_tn(nrm[...], sn[...])
         own_out(c).wait()
 
-    def step(s, carry):
-        @pl.when(s < n_chunk)
-        def _():
-            first_half(s)
-
-        @pl.when(s >= LAG)
-        def _():
-            second_half(s - LAG)
-
-        return carry
-
-    lax.fori_loop(0, n_chunk + LAG, step, 0)
-
-    def unpack(c, carry):
+    def unpack(c):
         for k in range(1, n_head):
             pltpu.make_async_remote_copy(
                 src_ref=rin.at[c, me], dst_ref=rout.at[c, lax.rem(me + n_head - k, n_head)],
@@ -443,24 +613,115 @@
         for s in range(n_head):
             turned = dot_nt(eye_lanes, rout[c, s])
             for w in range(CW):
-                xv[c % 2, s, w] = turned[:, w * RW : w * RW + WT].astype(BF16)
+                xv[lax.rem(c, 2), s, w] = turned[:, w * RW : w * RW + WT].astype(BF16)
         sect_copy(c).start()
+
+    def step(s, carry):
+        @pl.when(s < n_chunk)
+        def _():
+            first_half(s)
+
+        if n_win is not None:
+            @pl.when(s == n_chunk - 1)
+            def _():
+                for f in feeds:
+                    f.start_pair()
+
+            @pl.when(s == n_chunk)
+            def _():
+                for f in feeds:
+                    f.start_plane()
+
+        @pl.when((s >= LAG) & (s < n_chunk + LAG))
+        def _():
+            second_half(s - LAG)
+
+        if n_win is not None:
+            @pl.when(s == n_chunk + LAG - 1)
+            def _():
+                for f in others:
+                    f.start_pair()
+                table_sums()
+                small_in[at_pair, 0:HEADS, :] = vector_rows()
+                small_pair().start()
+
+            @pl.when(s == n_chunk + LAG)
+            def _():
+                for f in feeds:
+                    f.start_near()
+                for f in others:
+                    f.start_plane()
+                small_pair().wait_recv()
+                small_in[at_plane + my_win] = small_in[at_pair] + small_in[at_pair + 1]
+                for k in range(1, n_win):
+                    small_plane(k).start()
+                for f in feeds:
+                    f.start_far()
+
+        @pl.when(s >= UNPACK_LAG)
+        def _():
+            unpack(s - UNPACK_LAG)
+
         return carry
 
-    lax.fori_loop(0, n_chunk, unpack, 0)
+    def vector_rows():
+        row = jnp.sum(sums[...], axis=0, keepdims=True)
+        return jnp.concatenate([row[:, r * DM : (r + 1) * DM] for r in range(O_END // DM)], axis=0)
+
+    def table_sums():
+        total = jnp.zeros((HEADS, 4 * LN), F32)
+        for row in range(WIN):
+            spread = jnp.zeros((WIN * HEADS, 2 * LN), F32)
+            whole = jnp.concatenate([ds_acc[:, row * WIN + col, :] for col in range(WIN)], axis=0)
+            for part in split3(whole):
+                spread = spread + dot_nt(part, pick)
+            for col in range(WIN):
+                off = offset_of(WT - 1) - offset_of(row * WIN + col)
+                piece = jnp.concatenate(
+                    [spread[col * HEADS : (col + 1) * HEADS], jnp.zeros((HEADS, 2 * LN), F32)], axis=1
+                )
+                total = total + pltpu.roll(piece, off, 1)
+        if n_win is None:
+            g_small[HEADS:, :] = total
+        else:
+            small_in[at_pair, HEADS:, :] = total
+
+    lax.fori_loop(0, n_chunk + UNPACK_LAG, step, 0)
     for c in range(max(0, n_chunk - 2), n_chunk):
         sect_copy(c).wait()
 
-    g_small[...] = jnp.sum(sums[...], axis=0, keepdims=True)
-    g_table[...] = jnp.zeros_like(g_table)
-    for row in range(WIN):
-        spread = jnp.zeros((WIN * HEADS, 2 * LN), F32)
-        whole = jnp.concatenate([ds_acc[:, row * WIN + col, :] for col in range(WIN)], axis=0)
-        for part in split3(whole):
-            spread = spread + dot_nt(part, pick)
-        for col in range(WIN):
-            off = offset_of(WT - 1) - offset_of(row * WIN + col)
-            g_table[:, off : off + 2 * LN] += spread[col * HEADS : (col + 1) * HEADS]
+    if n_win is None:
+        g_small[0:HEADS, :] = vector_rows()
+        table_sums()
+    else:
+        for f in others:
+            f.start_near()
+        for k in range(1, n_win):
+            small_plane(k, lax.rem(my_win + n_win - k, n_win)).wait_recv()
+        total = small_in[at_plane]
+        for w in range(1, n_win):
+            total = total + small_in[at_plane + w]
+        small_in[at_near] = total
+        small_near().start()
+        for f in feeds:
+            f.finish()
+        for f in others:
+            f.start_far()
+        small_near().wait_recv()
+        small_in[at_far] = small_in[at_near] + small_in[at_near + 1]
+        small_far().start()
+        for f in reversed(others):
+            f.finish()
+        small_far().wait_recv()
+        g_small[...] = small_in[at_far] + small_in[at_far + 1]
+        others[-1].finish_gather()
+        for f in feeds + others:
+            f.drain()
+        small_pair().wait_send()
+        for k in range(1, n_win):
+            small_plane(k).wait_send()
+        small_near().wait_send()
+        small_far().wait_send()
 
     def drain(c, carry):
         for k in range(1, n_head):
@@ -471,7 +732,7 @@
     lax.fori_loop(0, n_chunk, drain, 0)
 
 
-def run_kernel(n_head, n_chunk, share, args):
+def run_kernel(n_head, n_win, n_chunk, share, args):
     lanes = QUADS * share
     any_, vmem = pl.BlockSpec(memory_space=pl.ANY), pl.BlockSpec(memory_space=pltpu.VMEM)
     smem = pl.BlockSpec(memory_space=pltpu.SMEM)
@@ -483,17 +744,29 @@
     out_shape = [
         jax.ShapeDtypeStruct((windows, WT, DM), BF16),
         jax.ShapeDtypeStruct((n_head, n_chunk, CW, lanes, WT), BF16),
-        jax.ShapeDtypeStruct((DM, FF), F32),
-        jax.ShapeDtypeStruct((FF, DM), F32),
-        jax.ShapeDtypeStruct((DM, 3 * DM), F32),
-        jax.ShapeDtypeStruct((DM, DM), F32),
-        jax.ShapeDtypeStruct((WIDTH, DM), F32),
-        jax.ShapeDtypeStruct((1, O_END), F32),
-        jax.ShapeDtypeStruct((HEADS, 4 * LN), F32),
     ]
-    out_specs = [vmem, any_] + [vmem] * 7
     dma = pltpu.SemaphoreType.DMA
-    scratch = [
+    scratch = []
+    if n_win is None:
+        out_shape += [jax.ShapeDtypeStruct(m, F32) for m in MATRICES]
+    else:
+        devices, n_z = n_win * n_head, n_head // 2
+        scratch += [pltpu.VMEM(m, F32) for m in MATRICES]
+        shares = [(m // devices, cols) for m, cols in MATRICES]
+        out_shape += [jax.ShapeDtypeStruct(m, F32) for m in shares[:-1]]
+        out_shape += [jax.ShapeDtypeStruct((shares[-1][0] * n_win, DM), F32)]
+        scratch += [pltpu.VMEM((rows * n_win * n_z, cols), BF16) for rows, cols in shares]
+        scratch += [pltpu.VMEM((n_win - 1, rows * n_z, cols), BF16) for rows, cols in shares]
+        scratch += [pltpu.VMEM((rows * (n_z // 2), cols), BF16) for rows, cols in shares]
+        scratch += [pltpu.VMEM((rows, cols), BF16) for rows, cols in shares]
+        scratch += [
+            pltpu.VMEM((n_win, shares[-1][0], DM), BF16),
+            pltpu.VMEM((n_win + 6, 2 * HEADS, DM), F32),
+            dma((6, 2 * n_win + 2)), dma((6, 2 * n_win + 2)),
+        ]
+    out_shape += [jax.ShapeDtypeStruct((2 * HEADS, DM), F32)]
+    out_specs = [vmem, any_] + [vmem] * 6
+    scratch += [
         pltpu.VMEM((2, n_head, CW, lanes, WT), BF16),
         pltpu.VMEM((n_chunk, n_head, R, lanes), BF16),
         pltpu.VMEM((n_chunk, n_head, R, lanes), BF16),
@@ -529,7 +802,7 @@
         dma((2,)), dma((6,)), dma, dma((2,)),
     ]
     return pl.pallas_call(
-        functools.partial(kernel, n_head, n_chunk, share),
+        functools.partial(kernel, n_head, n_win, n_chunk, share),
         out_shape=out_shape, in_specs=in_specs, out_specs=out_specs, scratch_shapes=scratch,
         compiler_params=pltpu.CompilerParams(
             collective_id=0, has_side_effects=True, vmem_limit_bytes=63 * 1024 * 1024
@@ -561,19 +834,26 @@
         jnp.pad(rel_table, ((0, 0), (0, 4 * LN - RELS))), proj_weight, row(proj_bias), row(norm2_gain), row(norm2_bias),
         fc1_weight, row(fc1_bias), fc2_weight, row(fc2_bias), window_valid, cotangent,
     )
-    block_out, section, fc1, fc2, qkv, proj, red, small, table = run_kernel(n_head, n_chunk, share, args)
+    n_win = lax.axis_size("win")
+    devices = n_win * n_head
+    inside = n_head == 8 and all((m // devices) % 16 == 0 for m, unused in MATRICES)
+    block_out, section, fc1, fc2, qkv, proj, red, small = run_kernel(
+        n_head, n_win if inside else None, n_chunk, share, args
+    )
     section_grad = section.reshape(group_windows, quads, share, tokens).transpose(0, 3, 1, 2)
     both = ("win", "head")
 
     def scattered(v):
         return lax.psum_scatter(v.astype(BF16), both, scatter_dimension=0, tiled=True).astype(F32)
 
-    mine = lax.psum_scatter(red.astype(BF16), "head", scatter_dimension=0, tiled=True)
-    reduce_grad = lax.psum(mine, "win").astype(F32).reshape(quads, share, DM)
-    vectors, table_grad = lax.psum((small[0], table), both)
-    table_grad = table_grad[:, :RELS]
+    if not inside:
+        fc1, fc2, qkv, proj = scattered(fc1), scattered(fc2), scattered(qkv), scattered(proj)
+        red = lax.psum_scatter(red.astype(BF16), "head", scatter_dimension=0, tiled=True)
+        red = lax.psum(red, "win").astype(F32)
+        small = lax.psum(small, both)
+    reduce_grad = red.reshape(quads, share, DM)
+    vectors, table_grad = small[:HEADS].reshape(-1), small[HEADS:, :RELS]
     at = lax.axis_index("win") * n_head + lax.axis_index("head")
-    devices = lax.axis_size("win") * n_head
 
     def part(start, length):
         size = length // devices
@@ -584,9 +864,10 @@
 
     return (
         block_out, section_grad, reduce_grad, part0(O_N0G), part0(O_N0B), part(O_N1G, DM), part(O_N1B, DM),
-        scattered(qkv), part(O_QB, DM), part(O_VB, DM), table_grad, scattered(proj), part(O_PB, DM),
-        part(O_N2G, DM), part(O_N2B, DM), scattered(fc1), part(O_FC1B, FF), scattered(fc2), part(O_FC2B, DM),
+        qkv, part(O_QB, DM), part(O_VB, DM), table_grad, proj, part(O_PB, DM),
+        part(O_N2G, DM), part(O_N2B, DM), fc1, part(O_FC1B, FF), fc2, part(O_FC2B, DM),
     )
+
 
 def solution(mesh):
     in_specs = (

time: 716 us -> 187 us (0.26)
  waiting for transfers between devices: 522 us -> 0 us
  Pallas kernels: 142 us -> 166 us
  other arithmetic: 21.5 us -> 0 us
  between operations: 15.3 us -> 0.7 us
    reduce_scatter x5 -> x0, waiting for transfers between devices: 436 us -> none  [the longest x4 402 us: scattered(): lax.psum_scatter(v.astype(BF16), both, scatter_dimension=0, tiled=True)]
    psum x2 -> x0, waiting for transfers between devices: 85.8 us -> none  [the longest x1 85.8 us: local(): vectors, table_grad = lax.psum((small[0], table), both)]
    pallas_call x1, Pallas kernels: 142 us -> 166 us  [run_kernel(): pl.pallas_call(functools.partial(kernel, n_head, n_win, n_chunk, share),...]
    convert_element_type x9 -> x0, other arithmetic: 19.9 us -> none  [the longest x4 11.4 us: scattered(): v.astype(BF16)]
  transfers between devices with their start and end apart: 7 -> 0, of which waited for: 6 -> 0; matrix products, arithmetic and copies ran while one was open for 3% -> 0% of each run, Pallas kernels for 0% -> 0%
where the time goes in v2:
time: 187 us; the launch traced here: 186 us
  Pallas kernels  166 us (89%)
  local copies, waits for them, and re-layouts  19.4 us (10%)
    pallas_call x1, Pallas kernels, run_kernel(): pl.pallas_call(functools.partial(kernel, n_head, n_win, n_chunk, share),...  166 us
    unnamed x19, local copies, waits for them, and re-layouts  11.2 us

profile of v2, /device:TPU:0, one launch (start us, length us, event | category | flops | bytes accessed | tf_op | source)
XLA Modules:
  0.0 186.4 jit_solution(4984321863175608971)
XLA Ops:
  0.7 0.8 reshape.100
  1.4 0.7 reshape.101.n0g
  2.1 0.8 reshape.102
  2.9 0.7 reshape.103.n0b
  3.6 1.4 pad.4.table
  4.9 166.3 %shard_map.339 = (bf16[12,100,512]{2,1,0:T(8,128)(2,1)}, bf16[8,6,2,128,100]{4,3,2,1,0:T(8,128)(2,1)}, f32[16,2048]{1,0:T(8,128)}, f32[64,512]{1,0:T(8,128)}, f3...) custom-call(bf16[8,6,2,128,100]{4,3,2,1,0:T(8,128)(2,1)} %bitcast.33, ...), custom_call_target="tpu_custom_call" | custom-call | flops 27000000512 | bytes 30000000 | tf_op jit(solution)/shard_map/pallas_call | solution.py:804
  171.2 0.8 slice_bitcast_fusion
  172.0 0.6 fusion
  172.6 0.1 fusion.1
  172.7 0.7 reshape.116
  173.4 0.7 reshape.117
  174.0 0.6 dynamic_slice.42
  174.6 1.3 slice.7
  176.0 2.4 %copy.53 = bf16[12,100,512]{2,1,0:T(8,128)(2,1)} copy(bf16[12,100,512]{2,1,0:T(8,128)(2,1)} %get-tuple-element.64) | data formatting | bytes 2457600
  178.4 0.0 copy-start.1
  178.4 4.7 %copy.54 = bf16[96,100,4,32]{1,3,2,0:T(8,128)(2,1)} copy(bf16[96,100,4,32]{1,3,2,0:T(8,128)(2,1)} %bitcast.26) | data formatting | bytes 4915200
  183.1 0.0 copy-done
  183.1 0.7 copy.55
  183.8 0.0 copy-done.3
  183.8 0.6 copy.56
  184.4 0.0 copy-done.4
  184.4 0.6 copy.57
  185.1 0.7 copy.58
  185.7 0.7 copy.59
  (9 shorter events, 0.0 us)
Async XLA Ops:
  178.4 4.7 %copy-start = (f32[128,512]{1,0:T(8,128)S(1)}, f32[128,512]{1,0:T(8,128)}, u32[]{:S(2)}) copy-start(f32[128,512]{1,0:T(8,128)} %get-tuple-element.29) | copy-start | bytes 786436
  178.4 5.4 %copy-start.3 = (f32[16,1536]{1,0:T(8,128)S(1)}, f32[16,1536]{1,0:T(8,128)}, u32[]{:S(2)}) copy-start(f32[16,1536]{1,0:T(8,128)} %get-tuple-element.71) | copy-start | bytes 294916
  178.4 6.0 %copy-start.4 = (f32[16,512]{1,0:T(8,128)S(1)}, f32[16,512]{1,0:T(8,128)}, u32[]{:S(2)}) copy-start(f32[16,512]{1,0:T(8,128)} %get-tuple-element.75) | copy-start | bytes 98308
  178.4 6.7 %copy-start.2 = (f32[16,2048]{1,0:T(8,128)S(1)}, f32[16,2048]{1,0:T(8,128)}, u32[]{:S(2)}) copy-start(f32[16,2048]{1,0:T(8,128)} %get-tuple-element.79) | copy-start | bytes 393220
  178.4 7.3 %copy-start.1 = (f32[64,512]{1,0:T(8,128)S(1)}, f32[64,512]{1,0:T(8,128)}, u32[]{:S(2)}) copy-start(f32[64,512]{1,0:T(8,128)} %get-tuple-element.81) | copy-start | bytes 393220

commit v3 on v2

--- a/solution.py
+++ b/solution.py
@@ -26,9 +26,9 @@
 LN = 128
 GROUPS = 4
 PER = 4
-LAG = 3
+LAG = 4
 SLOTS = LAG + 1
-UNPACK_LAG = LAG + 2
+AHEAD = 2
 RB = 16
 TILE = 512
 EPS = 1e-05
@@ -76,6 +76,13 @@
     for r in range(8, v.shape[0], 8):
         total = total + v[r : r + 8]
     return total
+
+
+def weave(one, two):
+    marks = [((i + 0.5) / len(one), piece) for i, piece in enumerate(one)]
+    marks += [((i + 0.5) / len(two), piece) for i, piece in enumerate(two)]
+    for unused, piece in sorted(marks, key=lambda m: m[0]):
+        piece()
 
 
 def gelu_parts(x):
@@ -116,9 +123,10 @@
         near_in, refs = refs[:5], refs[5:]
         far_in, refs = refs[:5], refs[5:]
         (gather_in, small_in, sum_send, sum_recv), refs = refs[:4], refs[4:]
-    (xv, send_in, rin, rout, wp, wqkv, wproj, wfc1, wfc2, cot,
-    nrm, res, fst, qkv, prob, att, stage, sec, sn, dy, wide, act, dh, ffo, dsn, dsec, dpk, d_heads, sums, bias_t, ds_acc,
-    in_send, in_recv, out_send, out_recv, x_sem, w_sem, own_sem, sect_sem) = refs
+    (xv, send_in, rin, wp, wqkv, wproj, wfc1, wfc2, cot,
+    nrm, res, fst, qkv, prob, att, stage, sec, sn, dy, wide, slim, ffo, dsn, dsec, dpk, d_heads, owns, out_stage, sums, bias_t, ds_acc,
+    in_send, in_recv, out_send, out_recv, x_sem, w_sem, cot_sem, own_sem, sect_sem, free_sem, done_sem) = refs
+    rout = send_in
     me = lax.axis_index("head")
     lanes = QUADS * share
 
@@ -314,6 +322,12 @@
     def x_copy(c):
         return pltpu.make_async_copy(x_hbm.at[:, c], xv.at[c % 2], x_sem.at[c % 2])
 
+    def cot_copy(c):
+        return pltpu.make_async_copy(cot_hbm.at[pl.ds(c * CW, CW)], cot.at[lax.rem(c, 2)], cot_sem.at[lax.rem(c, 2)])
+
+    def done_copy(c):
+        return pltpu.make_async_copy(out_stage.at[lax.rem(c, 2)], out_ref.at[pl.ds(c * CW, CW)], done_sem.at[lax.rem(c, 2)])
+
     def sect_copy(c):
         return pltpu.make_async_copy(xv.at[c % 2], sect_hbm.at[:, c], sect_sem.at[c % 2])
 
@@ -322,7 +336,6 @@
         pltpu.make_async_copy(wproj_hbm, wproj, w_sem.at[2]),
         pltpu.make_async_copy(wfc1_hbm, wfc1, w_sem.at[3]),
         pltpu.make_async_copy(wfc2_hbm, wfc2, w_sem.at[4]),
-        pltpu.make_async_copy(cot_hbm, cot, w_sem.at[5]),
     ]
 
     for c in range(min(2, n_chunk)):
@@ -340,13 +353,14 @@
             ).start()
     for w in weights:
         w.start()
-
-    eye_rows = (
-        lax.broadcasted_iota(jnp.int32, (RW, WT), 0) == lax.broadcasted_iota(jnp.int32, (RW, WT), 1)
-    ).astype(F32).astype(BF16)
-    eye_lanes = (
-        lax.broadcasted_iota(jnp.int32, (lanes, lanes), 0) == lax.broadcasted_iota(jnp.int32, (lanes, lanes), 1)
-    ).astype(F32).astype(BF16)
+    cot_copy(0).start()
+
+    def eye(rows, cols):
+        spot = lax.broadcasted_iota(jnp.int32, (rows, cols), 0) - lax.broadcasted_iota(jnp.int32, (rows, cols), 1)
+        return (spot == 0).astype(F32).astype(BF16)
+
+    eye_rows, eye_lanes = eye(RW, WT), eye(lanes, lanes)
+    eye_tokens, eye_heads = eye(RW, LN), eye(LN, LN)
 
     def repack(c):
         x_copy(c).wait()
@@ -370,7 +384,11 @@
             x_copy(c + 1).start()
 
         repack(c)
-        send(c)
+
+        @pl.when(c < AHEAD)
+        def _():
+            send(c)
+
         return carry
 
     lax.fori_loop(1, n_chunk, send_rest, 0)
@@ -432,6 +450,11 @@
                 device_id={"head": peer(k)}, device_id_type=MESH,
             )
             in_copy_wait.wait_recv()
+
+        @pl.when(c + AHEAD < n_chunk)
+        def _():
+            send(c + AHEAD)
+
         for r in range(0, R, RB):
             xhat, unused = normalised(merged_rows(c, r))
             nrm[r : r + RB, :] = (xhat * n0g[...] + n0b[...]).astype(BF16)
@@ -452,19 +475,19 @@
 
         def attend(w, carry):
             for g in range(GROUPS):
-                scores = dot_nt(qkv[p, w, 1, g, 0:JP, :], by_head(qkv[p, w, 0, g]))
-                found = []
+                wide[0, g * JP : (g + 1) * JP, :] = dot_nt(qkv[p, w, 1, g, 0:JP, :], by_head(qkv[p, w, 0, g]))
+            for g in range(GROUPS):
                 for h in range(PER):
-                    s = scores[:, h * LN : (h + 1) * LN] * (SCALE * LOG2E) + bias_t[g * PER + h]
+                    lane_h = slice(h * LN, (h + 1) * LN)
+                    s = wide[0, g * JP : (g + 1) * JP, lane_h] * (SCALE * LOG2E) + bias_t[g * PER + h]
                     e = jnp.exp2(s - jnp.max(s, axis=0, keepdims=True))
-                    found.append((e * (1.0 / jnp.sum(e, axis=0, keepdims=True))).astype(BF16))
-                probs = jnp.concatenate(found, axis=1)
-                prob[p, w, g] = probs
-                mixed = dot_tn(qkv[p, w, 2, g, 0:JP, :], probs)
-                own = jnp.concatenate(
-                    [mixed[h * HD : (h + 1) * HD, h * LN : (h + 1) * LN] for h in range(PER)], axis=0
-                )
-                stage[pl.ds(pl.multiple_of(w * RW, 8), RW), g * LN : (g + 1) * LN] = own.T[0:RW]
+                    prob[p, w, g, :, lane_h] = (e * (1.0 / jnp.sum(e, axis=0, keepdims=True))).astype(BF16)
+            for g in range(GROUPS):
+                mixed = dot_tn(qkv[p, w, 2, g, 0:JP, :], prob[p, w, g])
+                for h in range(PER):
+                    owns[g, h * HD : (h + 1) * HD, :] = mixed[h * HD : (h + 1) * HD, h * LN : (h + 1) * LN]
+            for g in range(GROUPS):
+                stage[pl.ds(pl.multiple_of(w * RW, 8), RW), g * LN : (g + 1) * LN] = owns[g].T[0:RW]
             return carry
 
         lax.fori_loop(0, CW, attend, 0)
@@ -473,38 +496,93 @@
         for r in range(0, R, RB):
             xhat, unused = normalised(sec[r : r + RB, :])
             sn[r : r + RB, :] = (xhat * n2g[...] + n2b[...]).astype(BF16)
+        cot_copy(c).wait()
+
+        @pl.when(c + 1 < n_chunk)
+        def _():
+            cot_copy(c + 1).start()
+
         flags = [valid[c * CW + w].astype(F32) for w in range(CW)]
         tail = jnp.zeros((RW - WT, DM), F32)
         pieces = []
         for w in range(CW):
-            pieces += [cot[c * CW + w].astype(F32) * flags[w], tail]
+            pieces += [cot[lax.rem(c, 2), w].astype(F32) * flags[w], tail]
         up = jnp.concatenate(pieces, axis=0)
         dy[...] = up.astype(BF16)
         sums[:, O_FC2B : O_FC2B + DM] += fold(up)
         ffo[...] = sec[...] + fc2b[...]
         dsn[...] = jnp.zeros_like(dsn)
 
-        def feed(t, carry):
-            cols = pl.ds(pl.multiple_of(t * TILE, TILE), TILE)
-            wide[:, 0:TILE] = dot(sn[...], wfc1[:, cols]) + fc1b[:, cols]
-            wide[:, TILE : 2 * TILE] = dot_nt(dy[...], wfc2[cols, :])
-            total = jnp.zeros((8, TILE), F32)
+        def spread(t):
+            b, half = t % 2, TILE // 2
+            for n in range(2):
+                cols = slice(t * TILE + n * half, t * TILE + (n + 1) * half)
+                into = slice(n * half, (n + 1) * half)
+
+                def one(cols=cols, into=into):
+                    wide[b, 0:R, into] = dot(sn[...], wfc1[:, cols]) + fc1b[:, cols]
+
+                def two(cols=cols, into=into):
+                    wide[b, R : 2 * R, into] = dot_nt(dy[...], wfc2[cols, :])
+
+                yield one
+                yield two
+
+        def bend(t):
+            b = t % 2
+            at = slice(O_FC1B + t * TILE, O_FC1B + (t + 1) * TILE)
             for r in range(0, R, RB):
-                value, slope = gelu_parts(wide[r : r + RB, 0:TILE])
-                act[r : r + RB, :] = value.astype(BF16)
-                low = (wide[r : r + RB, TILE : 2 * TILE] * slope).astype(BF16)
-                dh[r : r + RB, :] = low
-                total = total + fold(low.astype(F32))
-            sums[:, pl.ds(pl.multiple_of(O_FC1B + t * TILE, TILE), TILE)] += total
-            ffo[...] += dot(act[...], wfc2[cols, :])
-            dsn[...] += dot_nt(dh[...], wfc1[:, cols])
-            g_fc2[cols, :] += dot_tn(act[...], dy[...])
-            g_fc1[:, cols] += dot_tn(sn[...], dh[...])
-            return carry
-
-        lax.fori_loop(0, FF // TILE, feed, 0)
+
+                def one(r=r):
+                    value, slope = gelu_parts(wide[b, r : r + RB, :])
+                    slim[b, r : r + RB, :] = value.astype(BF16)
+                    low = (wide[b, R + r : R + r + RB, :] * slope).astype(BF16)
+                    slim[b, R + r : R + r + RB, :] = low
+                    sums[:, at] += fold(low.astype(F32))
+
+                yield one
+
+        def gather(t):
+            b, half = t % 2, TILE // 2
+            cols = slice(t * TILE, (t + 1) * TILE)
+            for n in range(2):
+                into = slice(n * half, (n + 1) * half)
+
+                def one(into=into):
+                    ffo[:, into] += dot(slim[b, 0:R, :], wfc2[cols, into])
+
+                def two(into=into):
+                    dsn[:, into] += dot_nt(slim[b, R : 2 * R, :], wfc1[into, cols])
+
+                yield one
+                yield two
+            for n in range(4):
+                lanes_n = slice(n * LN, (n + 1) * LN)
+                rows_n = slice(t * TILE + n * LN, t * TILE + (n + 1) * LN)
+
+                def one(lanes_n=lanes_n, rows_n=rows_n):
+                    g_fc2[rows_n, :] += dot_tn(slim[b, 0:R, lanes_n], dy[...])
+
+                def two(lanes_n=lanes_n):
+                    g_fc1[lanes_n, cols] += dot_tn(sn[:, lanes_n], slim[b, R : 2 * R, :])
+
+                yield one
+                yield two
+
+        tiles = FF // TILE
+        for piece in spread(0):
+            piece()
+        for t in range(tiles + 1):
+            heavy = (list(gather(t - 1)) if t else []) + (list(spread(t + 1)) if t + 1 < tiles else [])
+            light = list(bend(t)) if t < tiles else []
+            weave(heavy, light)
+        @pl.when(c >= 2)
+        def _():
+            done_copy(c - 2).wait()
+
         for w in range(CW):
-            out_ref[c * CW + w] = (ffo[w * RW : w * RW + WT, :] * flags[w]).astype(BF16)
+            out_stage[lax.rem(c, 2), w] = (ffo[w * RW : w * RW + WT, :] * flags[w]).astype(BF16)
+        done_copy(c).start()
         sum_g = jnp.zeros((8, DM), F32)
         sum_b = jnp.zeros((8, DM), F32)
         for r in range(0, R, RB):
@@ -529,29 +607,27 @@
                 d_heads[w, g, 0:JP, :] = padded(piece).astype(BF16)
 
         def attend(w, carry):
+            rows = pl.ds(pl.multiple_of(w * RW, 8), RW)
             for g in range(GROUPS):
-                d_out = by_head(d_heads[w, g])
-                q_all = by_head(qkv[p, w, 0, g])
-                d_probs = dot_nt(qkv[p, w, 2, g, 0:JP, :], d_out)
-                raw = []
+                wide[0, g * JP : (g + 1) * JP, :] = dot_nt(qkv[p, w, 2, g, 0:JP, :], by_head(d_heads[w, g]))
+            for g in range(GROUPS):
+                stage[rows, 2 * DM + g * LN : 2 * DM + (g + 1) * LN] = dot(prob[p, w, g], by_head(d_heads[w, g]))[0:RW]
+            for g in range(GROUPS):
                 for h in range(PER):
-                    pr = prob[p, w, g, :, h * LN : (h + 1) * LN].astype(F32)
-                    dp = d_probs[:, h * LN : (h + 1) * LN]
-                    pd = pr * dp
+                    lane_h = slice(h * LN, (h + 1) * LN)
+                    pr = prob[p, w, g, :, lane_h].astype(F32)
+                    pd = pr * wide[0, g * JP : (g + 1) * JP, lane_h]
                     d_s = pd - pr * jnp.sum(pd, axis=0, keepdims=True)
                     ds_acc[g * PER + h] += d_s
-                    raw.append((d_s * SCALE).astype(BF16))
-                d_raw = jnp.concatenate(raw, axis=1)
-                rows = pl.ds(pl.multiple_of(w * RW, 8), RW)
-                d_v = dot(prob[p, w, g], d_out)
-                d_k = dot(d_raw, q_all)
-                mixed = dot_tn(qkv[p, w, 1, g, 0:JP, :], d_raw)
-                own = jnp.concatenate(
-                    [mixed[h * HD : (h + 1) * HD, h * LN : (h + 1) * LN] for h in range(PER)], axis=0
-                )
-                stage[rows, g * LN : (g + 1) * LN] = own.T[0:RW]
-                stage[rows, DM + g * LN : DM + (g + 1) * LN] = d_k[0:RW]
-                stage[rows, 2 * DM + g * LN : 2 * DM + (g + 1) * LN] = d_v[0:RW]
+                    slim[0, g * JP : (g + 1) * JP, lane_h] = (d_s * SCALE).astype(BF16)
+            for g in range(GROUPS):
+                mixed = dot_tn(qkv[p, w, 1, g, 0:JP, :], slim[0, g * JP : (g + 1) * JP, :])
+                for h in range(PER):
+                    owns[g, h * HD : (h + 1) * HD, :] = mixed[h * HD : (h + 1) * HD, h * LN : (h + 1) * LN]
+            for g in range(GROUPS):
+                stage[rows, DM + g * LN : DM + (g + 1) * LN] = dot(slim[0, g * JP : (g + 1) * JP, :], by_head(qkv[p, w, 0, g]))[0:RW]
+            for g in range(GROUPS):
+                stage[rows, g * LN : (g + 1) * LN] = owns[g].T[0:RW]
             return carry
 
         lax.fori_loop(0, CW, attend, 0)
@@ -577,13 +653,14 @@
             sn[r : r + RB, :] = d_res.astype(BF16)
         sums[:, O_N1G : O_N1G + DM] += sum_g
         sums[:, O_N1B : O_N1B + DM] += sum_b
-        wide[...] = dot_nt(sn[...], wp[...])
+        wide[0, 0:R, :] = dot_nt(sn[...], wp[0:DM, :])
+        wide[0, R : 2 * R, :] = dot_nt(sn[...], wp[DM:WIDTH, :])
         sum_g = jnp.zeros((8, WIDTH), F32)
         sum_b = jnp.zeros((8, WIDTH), F32)
         for r in range(0, R, RB):
             xhat, inv = normalised(merged_rows(c, r))
             nrm[r : r + RB, :] = (xhat * n0g[...] + n0b[...]).astype(BF16)
-            d_out = wide[r : r + RB, :]
+            d_out = jnp.concatenate([wide[0, r : r + RB, :], wide[0, R + r : R + r + RB, :]], axis=1)
             sum_g = sum_g + fold(d_out * xhat)
             sum_b = sum_b + fold(d_out)
             low = norm_back(d_out, n0g[...], xhat, inv).astype(BF16)
@@ -616,6 +693,11 @@
                 xv[lax.rem(c, 2), s, w] = turned[:, w * RW : w * RW + WT].astype(BF16)
         sect_copy(c).start()
 
+    def sent(c, carry):
+        for k in range(1, n_head):
+            in_copy(c, k).wait_send()
+        return carry
+
     def step(s, carry):
         @pl.when(s < n_chunk)
         def _():
@@ -632,7 +714,14 @@
                 for f in feeds:
                     f.start_plane()
 
-        @pl.when((s >= LAG) & (s < n_chunk + LAG))
+        @pl.when(s == LAG)
+        def _():
+            lax.fori_loop(0, n_chunk, sent, 0)
+            for k in range(1, n_head):
+                pl.semaphore_signal(free_sem, inc=1, device_id={"head": peer(k)}, device_id_type=MESH)
+            pl.semaphore_wait(free_sem, n_head - 1)
+
+        @pl.when(s >= LAG)
         def _():
             second_half(s - LAG)
 
@@ -644,23 +733,6 @@
                 table_sums()
                 small_in[at_pair, 0:HEADS, :] = vector_rows()
                 small_pair().start()
-
-            @pl.when(s == n_chunk + LAG)
-            def _():
-                for f in feeds:
-                    f.start_near()
-                for f in others:
-                    f.start_plane()
-                small_pair().wait_recv()
-                small_in[at_plane + my_win] = small_in[at_pair] + small_in[at_pair + 1]
-                for k in range(1, n_win):
-                    small_plane(k).start()
-                for f in feeds:
-                    f.start_far()
-
-        @pl.when(s >= UNPACK_LAG)
-        def _():
-            unpack(s - UNPACK_LAG)
 
         return carry
 
@@ -686,16 +758,32 @@
         else:
             small_in[at_pair, HEADS:, :] = total
 
-    lax.fori_loop(0, n_chunk + UNPACK_LAG, step, 0)
-    for c in range(max(0, n_chunk - 2), n_chunk):
-        sect_copy(c).wait()
+    lax.fori_loop(0, n_chunk + LAG, step, 0)
+
+    def unpack_range(low, high):
+        def body(c, carry):
+            unpack(c)
+            return carry
+
+        lax.fori_loop(low, high, body, 0)
 
     if n_win is None:
         g_small[0:HEADS, :] = vector_rows()
         table_sums()
+        unpack_range(0, n_chunk)
     else:
         for f in others:
+            f.start_plane()
+        small_pair().wait_recv()
+        small_in[at_plane + my_win] = small_in[at_pair] + small_in[at_pair + 1]
+        for k in range(1, n_win):
+            small_plane(k).start()
+        for f in feeds:
             f.start_near()
+        unpack_range(0, n_chunk - 4)
+        for f in feeds:
+            f.start_far()
+        unpack_range(n_chunk - 4, n_chunk - 3)
         for k in range(1, n_win):
             small_plane(k, lax.rem(my_win + n_win - k, n_win)).wait_recv()
         total = small_in[at_plane]
@@ -703,17 +791,21 @@
             total = total + small_in[at_plane + w]
         small_in[at_near] = total
         small_near().start()
+        for f in others:
+            f.start_near()
         for f in feeds:
             f.finish()
-        for f in others:
-            f.start_far()
         small_near().wait_recv()
         small_in[at_far] = small_in[at_near] + small_in[at_near + 1]
         small_far().start()
+        for f in others:
+            f.start_far()
+        unpack_range(n_chunk - 3, n_chunk - 1)
         for f in reversed(others):
             f.finish()
         small_far().wait_recv()
         g_small[...] = small_in[at_far] + small_in[at_far + 1]
+        unpack_range(n_chunk - 1, n_chunk)
         others[-1].finish_gather()
         for f in feeds + others:
             f.drain()
@@ -722,10 +814,12 @@
             small_plane(k).wait_send()
         small_near().wait_send()
         small_far().wait_send()
+    for c in range(max(0, n_chunk - 2), n_chunk):
+        sect_copy(c).wait()
+        done_copy(c).wait()
 
     def drain(c, carry):
         for k in range(1, n_head):
-            in_copy(c, k).wait_send()
             out_copy(c, k).wait_send()
         return carry
 
@@ -765,10 +859,9 @@
             dma((6, 2 * n_win + 2)), dma((6, 2 * n_win + 2)),
         ]
     out_shape += [jax.ShapeDtypeStruct((2 * HEADS, DM), F32)]
-    out_specs = [vmem, any_] + [vmem] * 6
+    out_specs = [any_, any_] + [vmem] * 6
     scratch += [
         pltpu.VMEM((2, n_head, CW, lanes, WT), BF16),
-        pltpu.VMEM((n_chunk, n_head, R, lanes), BF16),
         pltpu.VMEM((n_chunk, n_head, R, lanes), BF16),
         pltpu.VMEM((n_chunk, n_head, R, lanes), BF16),
         pltpu.VMEM((WIDTH, DM), BF16),
@@ -776,7 +869,7 @@
         pltpu.VMEM((DM, DM), BF16),
         pltpu.VMEM((DM, FF), BF16),
         pltpu.VMEM((FF, DM), BF16),
-        pltpu.VMEM((windows, WT, DM), BF16),
+        pltpu.VMEM((2, CW, WT, DM), BF16),
         pltpu.VMEM((R, WIDTH), BF16),
         pltpu.VMEM((SLOTS, R, DM), F32),
         pltpu.VMEM((R, DM), BF16),
@@ -787,19 +880,20 @@
         pltpu.VMEM((R, DM), F32),
         pltpu.VMEM((R, DM), BF16),
         pltpu.VMEM((R, DM), BF16),
-        pltpu.VMEM((R, WIDTH), F32),
-        pltpu.VMEM((R, TILE), BF16),
-        pltpu.VMEM((R, TILE), BF16),
+        pltpu.VMEM((2, GROUPS * JP, TILE), F32),
+        pltpu.VMEM((2, GROUPS * JP, TILE), BF16),
         pltpu.VMEM((R, DM), F32),
         pltpu.VMEM((R, DM), F32),
         pltpu.VMEM((SLOTS, R, DM), F32),
         pltpu.VMEM((R, 3 * DM), BF16),
         pltpu.VMEM((CW, GROUPS, LN, LN), BF16),
+        pltpu.VMEM((GROUPS, LN, LN), F32),
+        pltpu.VMEM((2, CW, WT, DM), BF16),
         pltpu.VMEM((8, O_END), F32),
         pltpu.VMEM((HEADS, JP, LN), F32),
         pltpu.VMEM((HEADS, JP, LN), F32),
         dma((n_chunk, n_head)), dma((n_chunk, n_head)), dma((n_chunk, n_head)), dma((n_chunk, n_head)),
-        dma((2,)), dma((6,)), dma, dma((2,)),
+        dma((2,)), dma((5,)), dma((2,)), dma, dma((2,)), pltpu.SemaphoreType.REGULAR, dma((2,)),
     ]
     return pl.pallas_call(
         functools.partial(kernel, n_head, n_win, n_chunk, share),

time: 187 us -> 177 us (0.947)
  Pallas kernels: 166 us -> 155 us
    pallas_call x1, Pallas kernels: 166 us -> 155 us  [run_kernel(): pl.pallas_call(functools.partial(kernel, n_head, n_win, n_chunk, share),...]
where the time goes in v3:
time: 177 us; the launch traced here: 175 us
  Pallas kernels  155 us (88%)
  local copies, waits for them, and re-layouts  19.4 us (11%)
    pallas_call x1, Pallas kernels, run_kernel(): pl.pallas_call(functools.partial(kernel, n_head, n_win, n_chunk, share),...  155 us
    unnamed x19, local copies, waits for them, and re-layouts  11.2 us

profile of v3, /device:TPU:0, one launch (start us, length us, event | category | flops | bytes accessed | tf_op | source)
XLA Modules:
  0.0 175.1 jit_solution(12784715679298409677)
XLA Ops:
  0.7 0.8 reshape.100
  1.4 0.7 reshape.101.n0g
  2.1 0.8 reshape.102
  2.9 0.7 reshape.103.n0b
  3.6 1.4 pad.4.table
  4.9 155.0 %shard_map.339 = (bf16[12,100,512]{2,1,0:T(8,128)(2,1)}, bf16[8,6,2,128,100]{4,3,2,1,0:T(8,128)(2,1)}, f32[16,2048]{1,0:T(8,128)}, f32[64,512]{1,0:T(8,128)}, f3...) custom-call(bf16[8,6,2,128,100]{4,3,2,1,0:T(8,128)(2,1)} %bitcast.33, ...), custom_call_target="tpu_custom_call" | custom-call | flops 27000000512 | bytes 30000000 | tf_op jit(solution)/shard_map/pallas_call | solution.py:898
  159.9 0.8 slice_bitcast_fusion
  160.7 0.6 fusion
  161.3 0.1 fusion.1
  161.4 0.7 reshape.116
  162.1 0.7 reshape.117
  162.7 0.6 dynamic_slice.42
  163.3 1.3 slice.7
  164.7 2.4 %copy.53 = bf16[12,100,512]{2,1,0:T(8,128)(2,1)} copy(bf16[12,100,512]{2,1,0:T(8,128)(2,1)} %get-tuple-element.64) | data formatting | bytes 2457600
  167.1 0.0 copy-start.1
  167.1 4.7 %copy.54 = bf16[96,100,4,32]{1,3,2,0:T(8,128)(2,1)} copy(bf16[96,100,4,32]{1,3,2,0:T(8,128)(2,1)} %bitcast.26) | data formatting | bytes 4915200
  171.8 0.0 copy-done
  171.8 0.7 copy.55
  172.5 0.0 copy-done.3
  172.5 0.6 copy.56
  173.1 0.6 copy.57
  173.7 0.0 copy-done.2
  173.7 0.7 copy.58
  174.4 0.7 copy.59
  (9 shorter events, 0.0 us)
Async XLA Ops:
  167.1 4.7 %copy-start = (f32[128,512]{1,0:T(8,128)S(1)}, f32[128,512]{1,0:T(8,128)}, u32[]{:S(2)}) copy-start(f32[128,512]{1,0:T(8,128)} %get-tuple-element.29) | copy-start | bytes 786436
  167.1 5.4 %copy-start.3 = (f32[16,1536]{1,0:T(8,128)S(1)}, f32[16,1536]{1,0:T(8,128)}, u32[]{:S(2)}) copy-start(f32[16,1536]{1,0:T(8,128)} %get-tuple-element.71) | copy-start | bytes 294916
  167.1 6.0 %copy-start.4 = (f32[16,512]{1,0:T(8,128)S(1)}, f32[16,512]{1,0:T(8,128)}, u32[]{:S(2)}) copy-start(f32[16,512]{1,0:T(8,128)} %get-tuple-element.75) | copy-start | bytes 98308
  167.1 6.7 %copy-start.2 = (f32[16,2048]{1,0:T(8,128)S(1)}, f32[16,2048]{1,0:T(8,128)}, u32[]{:S(2)}) copy-start(f32[16,2048]{1,0:T(8,128)} %get-tuple-element.79) | copy-start | bytes 393220
  167.1 7.3 %copy-start.1 = (f32[64,512]{1,0:T(8,128)S(1)}, f32[64,512]{1,0:T(8,128)}, u32[]{:S(2)}) copy-start(f32[64,512]{1,0:T(8,128)} %get-tuple-element.81) | copy-start | bytes 393220

commit v4 on v3

--- a/solution.py
+++ b/solution.py
@@ -109,7 +109,7 @@
 
 def kernel(
     n_head, n_win, n_chunk, share,
-    x_hbm, wp_hbm, n0g, n0b, n1g, n1b, wqkv_hbm, qb, vb, table, wproj_hbm, pb, n2g, n2b,
+    x_hbm, wp_hbm, gain0, bias0, n1g, n1b, wqkv_hbm, qb, vb, table_in, wproj_hbm, pb, n2g, n2b,
     wfc1_hbm, fc1b, wfc2_hbm, fc2b, valid, cot_hbm,
     *refs,
 ):
@@ -124,7 +124,7 @@
         far_in, refs = refs[:5], refs[5:]
         (gather_in, small_in, sum_send, sum_recv), refs = refs[:4], refs[4:]
     (xv, send_in, rin, wp, wqkv, wproj, wfc1, wfc2, cot,
-    nrm, res, fst, qkv, prob, att, stage, sec, sn, dy, wide, slim, ffo, dsn, dsec, dpk, d_heads, owns, out_stage, sums, bias_t, ds_acc,
+    nrm, res, fst, qkv, prob, att, stage, sec, sn, dy, wide, slim, ffo, dsn, dsec, dpk, d_heads, n0g, n0b, table, owns, out_stage, sums, bias_t, ds_acc,
     in_send, in_recv, out_send, out_recv, x_sem, w_sem, cot_sem, own_sem, sect_sem, free_sem, done_sem) = refs
     rout = send_in
     me = lax.axis_index("head")
@@ -411,6 +411,13 @@
     d_heads[...] = jnp.zeros_like(d_heads)
     bias_t[:, WT:, :] = jnp.full((HEADS, JP - WT, LN), -1e30, F32)
 
+    for row, given in ((n0g, gain0), (n0b, bias0)):
+        for s in range(n_head):
+            row[:, s * lanes : (s + 1) * lanes] = jnp.concatenate(
+                [given[q : q + 1, s * share : (s + 1) * share] for q in range(QUADS)], axis=1
+            )
+    table[...] = jnp.zeros_like(table)
+    table[:, 0:RELS] = table_in[...]
     spot = lax.broadcasted_iota(jnp.int32, (2 * LN, LN), 0)
     token = lax.broadcasted_iota(jnp.int32, (2 * LN, LN), 1)
     token_row = (token * 205) >> 11
@@ -887,6 +894,9 @@
         pltpu.VMEM((SLOTS, R, DM), F32),
         pltpu.VMEM((R, 3 * DM), BF16),
         pltpu.VMEM((CW, GROUPS, LN, LN), BF16),
+        pltpu.VMEM((1, WIDTH), F32),
+        pltpu.VMEM((1, WIDTH), F32),
+        pltpu.VMEM((HEADS, 4 * LN), F32),
         pltpu.VMEM((GROUPS, LN, LN), F32),
         pltpu.VMEM((2, CW, WT, DM), BF16),
         pltpu.VMEM((8, O_END), F32),
@@ -905,6 +915,65 @@
     )(*args)
 
 
+def finish_kernel(n_head, devices, share, whole, *refs):
+    arrays, small, outs = refs[:whole], refs[whole], refs[whole + 1 : -2 - whole]
+    held, (in_sem, out_sem) = refs[-2 - whole : -2], refs[-2:]
+    arriving, leaving = [], []
+    for source, middle, target in zip(arrays, held, outs[:whole]):
+        pieces = source.shape[0] if len(source.shape) > 2 else 1
+        for i in range(pieces):
+            part = pl.ds(i, 1) if pieces > 1 else pl.ds(0, source.shape[0])
+            arriving.append(pltpu.make_async_copy(source.at[part], middle.at[part], in_sem.at[len(arriving)]))
+            leaving.append(pltpu.make_async_copy(middle.at[part], target.at[part], out_sem.at[len(leaving)]))
+    for copy in arriving:
+        copy.start()
+    n0g, n0b, n1g, n1b, qb, vb, table, pb, n2g, n2b, fc1b, fc2b = outs[whole:]
+    head = lax.axis_index("head")
+    at = lax.axis_index("win") * n_head + head
+
+    def taken(start, size, spot):
+        first = spot * size
+        row = small[pl.ds(start // DM + first // DM, 1), :]
+        return pltpu.roll(row, lax.rem(DM - lax.rem(first, DM), DM), 1)[:, 0:size]
+
+    for target, start in (
+        (n1g, O_N1G), (n1b, O_N1B), (qb, O_QB), (vb, O_VB), (pb, O_PB), (n2g, O_N2G), (n2b, O_N2B), (fc2b, O_FC2B),
+    ):
+        target[...] = taken(start, DM // devices, at)
+    fc1b[...] = taken(O_FC1B, FF // devices, at)
+    for target, start in ((n0g, O_N0G), (n0b, O_N0B)):
+        row = taken(start, QUADS * share, head)
+        for q in range(QUADS):
+            target[q : q + 1, :] = row[:, q * share : (q + 1) * share]
+    table[...] = small[HEADS:, 0:RELS]
+    for copy, onward in zip(arriving, leaving):
+        copy.wait()
+        onward.start()
+    for copy in leaving:
+        copy.wait()
+
+
+def run_finish(n_head, devices, share, args):
+    any_, vmem = pl.BlockSpec(memory_space=pl.ANY), pl.BlockSpec(memory_space=pltpu.VMEM)
+    block_out, section, red, qkv, proj, fc1, fc2, small = args
+    whole = (block_out, section, red, qkv, proj, fc1, fc2)
+    one, wide = (1, DM // devices), (1, FF // devices)
+    norm = (QUADS, share)
+    shapes = [(v.shape, v.dtype) for v in whole]
+    shapes += [(m, F32) for m in (norm, norm, one, one, one, one, (HEADS, RELS), one, one, one, wide, one)]
+    count = sum(v.shape[0] if v.ndim > 2 else 1 for v in whole)
+    outs = pl.pallas_call(
+        functools.partial(finish_kernel, n_head, devices, share, len(whole)),
+        out_shape=[jax.ShapeDtypeStruct(m, t) for m, t in shapes],
+        in_specs=[any_] * len(whole) + [vmem], out_specs=[any_] * len(whole) + [vmem] * 12,
+        scratch_shapes=[pltpu.VMEM(v.shape, v.dtype) for v in whole]
+        + [pltpu.SemaphoreType.DMA((count,)), pltpu.SemaphoreType.DMA((count,))],
+        compiler_params=pltpu.CompilerParams(vmem_limit_bytes=63 * 1024 * 1024),
+    )(*args)
+    block_out, section, red, qkv, proj, fc1, fc2, n0g, n0b, n1g, n1b, qb, vb, table, pb, n2g, n2b, fc1b, fc2b = outs
+    return block_out, section, red, n0g, n0b, n1g, n1b, qkv, qb, vb, table, proj, pb, n2g, n2b, fc1, fc1b, fc2, fc2b
+
+
 def local(
     n_head, section_rows, reduce_weight, norm0_gain, norm0_bias, norm1_gain, norm1_bias, qkv_weight, q_bias, v_bias,
     rel_table, proj_weight, proj_bias, norm2_gain, norm2_bias, fc1_weight, fc1_bias, fc2_weight, fc2_bias,
@@ -916,16 +985,13 @@
     lanes = quads * share
     rows = section_rows.transpose(0, 2, 3, 1).reshape(n_head, n_chunk, CW, lanes, tokens)
 
-    def by_source(v):
-        return v.reshape(quads, n_head, share).transpose(1, 0, 2).reshape(1, WIDTH)
-
     def row(v):
         return v.reshape(1, -1)
 
     args = (
-        rows, reduce_weight.reshape(quads, n_head, share, DM), by_source(norm0_gain), by_source(norm0_bias),
+        rows, reduce_weight.reshape(quads, n_head, share, DM), norm0_gain, norm0_bias,
         row(norm1_gain), row(norm1_bias), qkv_weight, row(q_bias), row(v_bias),
-        jnp.pad(rel_table, ((0, 0), (0, 4 * LN - RELS))), proj_weight, row(proj_bias), row(norm2_gain), row(norm2_bias),
+        rel_table, proj_weight, row(proj_bias), row(norm2_gain), row(norm2_bias),
         fc1_weight, row(fc1_bias), fc2_weight, row(fc2_bias), window_valid, cotangent,
     )
     n_win = lax.axis_size("win")
@@ -934,7 +1000,6 @@
     block_out, section, fc1, fc2, qkv, proj, red, small = run_kernel(
         n_head, n_win if inside else None, n_chunk, share, args
     )
-    section_grad = section.reshape(group_windows, quads, share, tokens).transpose(0, 3, 1, 2)
     both = ("win", "head")
 
     def scattered(v):
@@ -945,21 +1010,17 @@
         red = lax.psum_scatter(red.astype(BF16), "head", scatter_dimension=0, tiled=True)
         red = lax.psum(red, "win").astype(F32)
         small = lax.psum(small, both)
-    reduce_grad = red.reshape(quads, share, DM)
-    vectors, table_grad = small[:HEADS].reshape(-1), small[HEADS:, :RELS]
-    at = lax.axis_index("win") * n_head + lax.axis_index("head")
-
-    def part(start, length):
-        size = length // devices
-        return lax.dynamic_slice_in_dim(vectors, start + at * size, size)
-
-    def part0(start):
-        return lax.dynamic_slice_in_dim(vectors, start + lax.axis_index("head") * lanes, lanes).reshape(quads, share)
+    block_out, section, red, n0g, n0b, n1g, n1b, qkv, qb, vb, table, proj, pb, n2g, n2b, fc1, fc1b, fc2, fc2b = (
+        run_finish(n_head, devices, share, (block_out, section, red, qkv, proj, fc1, fc2, small))
+    )
+    section_grad = section.reshape(group_windows, quads, share, tokens).transpose(0, 3, 1, 2)
+
+    def flat(v):
+        return v.reshape(-1)
 
     return (
-        block_out, section_grad, reduce_grad, part0(O_N0G), part0(O_N0B), part(O_N1G, DM), part(O_N1B, DM),
-        qkv, part(O_QB, DM), part(O_VB, DM), table_grad, proj, part(O_PB, DM),
-        part(O_N2G, DM), part(O_N2B, DM), fc1, part(O_FC1B, FF), fc2, part(O_FC2B, DM),
+        block_out, section_grad, red.reshape(quads, share, DM), n0g, n0b, flat(n1g), flat(n1b), qkv, flat(qb), flat(vb),
+        table, proj, flat(pb), flat(n2g), flat(n2b), fc1, flat(fc1b), fc2, flat(fc2b),
     )
 
 

time: 177 us -> 163 us (0.921)
  local copies, waits for them, and re-layouts: 19.4 us -> 0 us
  Pallas kernels: 155 us -> 161 us
    unnamed x19 -> x0, local copies, waits for them, and re-layouts: 11.2 us -> none
    pallas_call x0 -> x1, Pallas kernels: none -> 6.4 us  [run_finish(): pl.pallas_call(functools.partial(finish_kernel, n_head, devices, share, l...]
    reshape x8 -> x0, local copies, waits for them, and re-layouts: 4.23 us -> none  [the longest x6 2.91 us: by_source(): return v.reshape(quads, n_head, share).transpose(1, 0, 2).reshape(1, WIDTH)]
where the time goes in v4:
time: 163 us; the launch traced here: 162 us
  Pallas kernels  161 us (99%)
    pallas_call x1, Pallas kernels, run_kernel(): pl.pallas_call(functools.partial(kernel, n_head, n_win, n_chunk, share),...  155 us
    pallas_call x1, Pallas kernels, run_finish(): pl.pallas_call(functools.partial(finish_kernel, n_head, devices, share, l...  6.4 us

profile of v4, /device:TPU:0, one launch (start us, length us, event | category | flops | bytes accessed | tf_op | source)
XLA Modules:
  0.0 162.1 jit_solution(14885555493286367694)
XLA Ops:
  0.7 154.8 %shard_map.339 = (bf16[12,100,512]{2,1,0:T(8,128)(2,1)}, bf16[8,6,2,128,100]{4,3,2,1,0:T(8,128)(2,1)}, f32[16,2048]{1,0:T(8,128)}, f32[64,512]{1,0:T(8,128)}, f3...) custom-call(bf16[8,6,2,128,100]{4,3,2,1,0:T(8,128)(2,1)} %bitcast.26, ...), custom_call_target="tpu_custom_call" | custom-call | flops 27000000512 | bytes 30000000 | tf_op jit(solution)/shard_map/pallas_call | solution.py:908
  155.5 6.4 %shard_map.340 = (bf16[12,100,512]{2,1,0:T(8,128)(2,1)}, bf16[8,6,2,128,100]{4,3,2,1,0:T(8,128)(2,1)}, f32[128,512]{1,0:T(8,128)}, f32[16,1536]{1,0:T(8,128)}, f...) custom-call(bf16[12,100,512]{2,1,0:T(8,128)(2,1)} %get-tuple-element, ...), custom_call_target="tpu_custom_call" | custom-call | tf_op jit(solution)/shard_map/pallas_call | solution.py:965

commit v5 on v4

--- a/solution.py
+++ b/solution.py
@@ -738,7 +738,7 @@
                 for f in others:
                     f.start_pair()
                 table_sums()
-                small_in[at_pair, 0:HEADS, :] = vector_rows()
+                small_in[at_pair, 0:HEADS, :] = vector_rows().astype(BF16)
                 small_pair().start()
 
         return carry
@@ -763,7 +763,7 @@
         if n_win is None:
             g_small[HEADS:, :] = total
         else:
-            small_in[at_pair, HEADS:, :] = total
+            small_in[at_pair, HEADS:, :] = total.astype(BF16)
 
     lax.fori_loop(0, n_chunk + LAG, step, 0)
 
@@ -782,7 +782,7 @@
         for f in others:
             f.start_plane()
         small_pair().wait_recv()
-        small_in[at_plane + my_win] = small_in[at_pair] + small_in[at_pair + 1]
+        small_in[at_plane + my_win] = (small_in[at_pair].astype(F32) + small_in[at_pair + 1].astype(F32)).astype(BF16)
         for k in range(1, n_win):
             small_plane(k).start()
         for f in feeds:
@@ -793,17 +793,17 @@
         unpack_range(n_chunk - 4, n_chunk - 3)
         for k in range(1, n_win):
             small_plane(k, lax.rem(my_win + n_win - k, n_win)).wait_recv()
-        total = small_in[at_plane]
+        total = small_in[at_plane].astype(F32)
         for w in range(1, n_win):
-            total = total + small_in[at_plane + w]
-        small_in[at_near] = total
+            total = total + small_in[at_plane + w].astype(F32)
+        small_in[at_near] = total.astype(BF16)
         small_near().start()
         for f in others:
             f.start_near()
         for f in feeds:
             f.finish()
         small_near().wait_recv()
-        small_in[at_far] = small_in[at_near] + small_in[at_near + 1]
+        small_in[at_far] = (small_in[at_near].astype(F32) + small_in[at_near + 1].astype(F32)).astype(BF16)
         small_far().start()
         for f in others:
             f.start_far()
@@ -811,7 +811,7 @@
         for f in reversed(others):
             f.finish()
         small_far().wait_recv()
-        g_small[...] = small_in[at_far] + small_in[at_far + 1]
+        g_small[...] = small_in[at_far].astype(F32) + small_in[at_far + 1].astype(F32)
         unpack_range(n_chunk - 1, n_chunk)
         others[-1].finish_gather()
         for f in feeds + others:
@@ -862,7 +862,7 @@
         scratch += [pltpu.VMEM((rows, cols), BF16) for rows, cols in shares]
         scratch += [
             pltpu.VMEM((n_win, shares[-1][0], DM), BF16),
-            pltpu.VMEM((n_win + 6, 2 * HEADS, DM), F32),
+            pltpu.VMEM((n_win + 6, 2 * HEADS, DM), BF16),
             dma((6, 2 * n_win + 2)), dma((6, 2 * n_win + 2)),
         ]
     out_shape += [jax.ShapeDtypeStruct((2 * HEADS, DM), F32)]

time: 163 us -> 161 us (0.988)
  Pallas kernels: 161 us -> 159 us
    pallas_call x1, Pallas kernels: 155 us -> 153 us  [run_kernel(): pl.pallas_call(functools.partial(kernel, n_head, n_win, n_chunk, share),...]
where the time goes in v5:
time: 161 us; the launch traced here: 160 us
  Pallas kernels  159 us (99%)
    pallas_call x1, Pallas kernels, run_kernel(): pl.pallas_call(functools.partial(kernel, n_head, n_win, n_chunk, share),...  153 us
    pallas_call x1, Pallas kernels, run_finish(): pl.pallas_call(functools.partial(finish_kernel, n_head, devices, share, l...  6.4 us

profile of v5, /device:TPU:0, one launch (start us, length us, event | category | flops | bytes accessed | tf_op | source)
XLA Modules:
  0.0 160.1 jit_solution(1643066345509645392)
XLA Ops:
  0.7 152.8 %shard_map.339 = (bf16[12,100,512]{2,1,0:T(8,128)(2,1)}, bf16[8,6,2,128,100]{4,3,2,1,0:T(8,128)(2,1)}, f32[16,2048]{1,0:T(8,128)}, f32[64,512]{1,0:T(8,128)}, f3...) custom-call(bf16[8,6,2,128,100]{4,3,2,1,0:T(8,128)(2,1)} %bitcast.26, ...), custom_call_target="tpu_custom_call" | custom-call | flops 27000000512 | bytes 30000000 | tf_op jit(solution)/shard_map/pallas_call | solution.py:908
  153.5 6.4 %shard_map.340 = (bf16[12,100,512]{2,1,0:T(8,128)(2,1)}, bf16[8,6,2,128,100]{4,3,2,1,0:T(8,128)(2,1)}, f32[128,512]{1,0:T(8,128)}, f32[16,1536]{1,0:T(8,128)}, f...) custom-call(bf16[12,100,512]{2,1,0:T(8,128)(2,1)} %get-tuple-element, ...), custom_call_target="tpu_custom_call" | custom-call | tf_op jit(solution)/shard_map/pallas_call | solution.py:965
